TPU v7x, 512 devices: a whole 4x4x16 slice. The times are simulated.
512 devices in a mesh: energy: 32 (over z, core), section: 16 (over y, x).
Axes of the slice: x: 4, y: 4, z: 16, core: 2. Of those that a mesh axis runs over, the one named last changes fastest.
Arguments:
- g_less: float32 [512, 16, 1024], P('energy', 'section'), may hold values from -6 to 6
- g_greater: float32 [512, 16, 1024], P('energy', 'section'), may hold values from -6 to 6
- partner: int32 [16, 1024], P('section'), may hold values from 0 to 1023, each once within a row
- pair_rows: int32 [16, 1024], P('section'), may hold values from 0 to 415
- pair_weight: float32 [16, 1024], P('section'), may hold values from -1.8 to 1.8
- source: float32 [16, 416], P('section'), may hold values from -6 to 6
- slab_inverse: float32 [16, 416, 416], P('section'), may hold values from -0.25 to 1.25
- coupling: float32 [16, 416, 416], P('section'), may hold values from -0.3125 to 0.3125
Outputs:
- sigma: float32 [512, 16, 1024], P(None, 'section', 'energy')
Inputs may be any that keep to these rules, and one draw needn't show every extreme that they name: `partner`: each slab's row lists every one of its 1024 pair columns once.
All inputs are finite; a program needn't handle non-finite values.
Results may differ from a plain program's by a relative error of at most 0.0003.
Values sent between devices are 32-bit elements; how exact they have to be, the bound alone decides.
A program may use at most 64 MiB of HBM per device.

v0:
```python
import functools
import math

import jax
import jax.numpy as jnp
import numpy as np
from jax import lax
from jax.experimental import pallas as pl
from jax.experimental.pallas import tpu as pltpu
from jax.sharding import PartitionSpec as P

MESH = pl.DeviceIdType.MESH
F32 = jnp.float32
BF16 = jnp.bfloat16
NT = (((1,), (1,)), ((), ()))
NN = (((1,), (0,)), ((), ()))
LENGTH = 768
HALF = LENGTH // 2


def two_parts(table):
    table = np.asarray(table, np.float32)
    high = table.astype(jnp.bfloat16)
    low = (table - high.astype(np.float32)).astype(jnp.bfloat16)
    return jnp.asarray(high), jnp.asarray(low)


def angles(times):
    return np.outer(np.arange(HALF) + 0.5, np.asarray(times, np.float64)) * (2.0 * math.pi / LENGTH)


def forward_table(order):
    phase = angles(order)
    return two_parts(np.concatenate([np.cos(phase), np.sin(phase)], axis=0))


def inverse_table(times, energies):
    phase = angles(times).T
    scale = 2.0 / LENGTH / math.sqrt(energies)
    return two_parts(np.concatenate([np.cos(phase), np.sin(phase)], axis=1) * scale)


def energy_order(peers, own, fold):
    rows = own // fold
    group, sender, row = np.meshgrid(np.arange(fold), np.arange(peers), np.arange(rows), indexing="ij")
    return (sender * own + group * rows + row).reshape(-1)


def lanes_of(shape):
    return lax.broadcasted_iota(jnp.int32, shape, len(shape) - 1)


def roll(x, shift, axis=1):
    return pltpu.roll(x, shift, axis)


def exchange_groups(parts):
    a0, a1, a2, a3 = parts
    lane = lanes_of(a0.shape)
    low = lane < 64
    near = lane % 64 < 32
    b0, b2 = jnp.where(low, a0, roll(a2, 64)), jnp.where(low, roll(a0, 64), a2)
    b1, b3 = jnp.where(low, a1, roll(a3, 64)), jnp.where(low, roll(a1, 64), a3)
    c0, c1 = jnp.where(near, b0, roll(b1, 32)), jnp.where(near, roll(b0, 96), b1)
    c2, c3 = jnp.where(near, b2, roll(b3, 32)), jnp.where(near, roll(b2, 96), b3)
    return c0, c1, c2, c3


def exchange_rows(first, second):
    lane = lanes_of(first.shape)
    row = lax.broadcasted_iota(jnp.int32, first.shape, 0)
    low = lane < 64
    upper_half = row < 4
    keep = (lane % 64 < 32) == upper_half
    one, two = jnp.where(low, first, roll(second, 64)), jnp.where(low, roll(first, 64), second)

    def inside(x):
        turned = roll(x, 4, 0)
        return jnp.where(keep, x, jnp.where(upper_half, roll(turned, 32), roll(turned, 96)))

    return inside(one), inside(two)


def split(x):
    high = x.astype(BF16)
    return high, (x - high.astype(F32)).astype(BF16)


def dot(x, y, dims=NN):
    return lax.dot_general(x, y, dims, preferred_element_type=F32)


def product(x, high, low, dims):
    rows = x.shape[0]
    x_high, x_low = split(x)
    both = dot(jnp.concatenate([x_high, x_low], axis=0), high, dims)
    return both[:rows] + both[rows:] + dot(x_high, low, dims)


def scatter_start(peers, me, source, target, send, recv):
    def one(k, _):
        peer = lax.rem(me + k, peers)
        pltpu.make_async_remote_copy(
            src_ref=source.at[peer],
            dst_ref=target.at[me],
            send_sem=send.at[k],
            recv_sem=recv.at[k],
            device_id={"energy": peer},
            device_id_type=MESH,
        ).start()
        return 0

    lax.fori_loop(1, peers, one, 0)
    target[me] = source[me]


def scatter_wait(peers, me, source, target, send, recv):
    def one(k, _):
        peer = lax.rem(me + k, peers)
        copy = pltpu.make_async_remote_copy(
            src_ref=source.at[peer],
            dst_ref=target.at[me],
            send_sem=send.at[k],
            recv_sem=recv.at[k],
            device_id={"energy": peer},
            device_id_type=MESH,
        )
        copy.wait_send()
        copy.wait_recv()
        return 0

    lax.fori_loop(1, peers, one, 0)


def lane_take(x, index):
    return jnp.take_along_axis(x, index, axis=1, mode="promise_in_bounds")


def main_kernel(
    peers, sections,
    less_ref, great_ref, partner_ref, rows_ref, weight_ref, source_ref, inverse_ref, coupling_ref,
    fwd_high, fwd_low, inv_high, inv_low,
    values_out, spectrum_out,
    swapped, first_send, first_recv, second_send, second_recv, third_send,
    tables, table_sem, orbital_table, slab_high, slab_low, couple_high, couple_low, map_high, map_low,
    upward, upper, carried_out, carried_in,
    send_one, recv_one, send_two, recv_two, send_three, recv_three, shift_sem, sweep_sem,
):
    me = lax.axis_index("energy")
    section = lax.axis_index("section")
    has_before = section > 0
    has_after = section < sections - 1
    before = lax.rem(section + sections - 1, sections)
    after = lax.rem(section + 1, sections)
    orbitals = inverse_ref.shape[0]

    barrier = pltpu.get_barrier_semaphore()

    def greet(k, _):
        pl.semaphore_signal(barrier, inc=1, device_id={"energy": lax.rem(me + k, peers)}, device_id_type=MESH)
        return 0

    lax.fori_loop(1, peers, greet, 0)

    @pl.when(has_before)
    def _():
        pl.semaphore_signal(barrier, inc=1, device_id={"section": before}, device_id_type=MESH)

    @pl.when(has_after)
    def _():
        pl.semaphore_signal(barrier, inc=1, device_id={"section": after}, device_id_type=MESH)

    loads = [
        pltpu.make_async_copy(ref, tables.at[place], table_sem.at[place])
        for place, ref in enumerate((fwd_high, fwd_low))
    ]
    for load in loads:
        load.start()

    partner = partner_ref[...]
    partner_tile, partner_lane = partner // 128, partner % 128
    for energy in range(16):
        total = jnp.zeros((8, 128), F32)
        for tile in range(8):
            line = jnp.broadcast_to(great_ref[8 * energy + tile : 8 * energy + tile + 1, :], (8, 128))
            total = jnp.where(partner_tile == tile, lane_take(line, partner_lane), total)
        swapped[8 * energy : 8 * energy + 8, :] = total

    for tile in range(8):
        parts = []
        for h in range(2):
            for ref in (less_ref, swapped):
                parts.append(ref[pl.ds(64 * h + tile, 8, stride=8), :])
        for b, part in enumerate(exchange_groups(parts)):
            first_send[4 * tile + b] = part

    pl.semaphore_wait(barrier, peers - 1 + has_before.astype(jnp.int32) + has_after.astype(jnp.int32))
    scatter_start(peers, me, first_send, first_recv, send_one, recv_one)

    pair_rows = rows_ref[...]
    for tile in range(8):
        index = lax.broadcasted_iota(jnp.int32, (orbitals, 128), 0)
        orbital_table[:, 128 * tile : 128 * tile + 128] = (
            (index == pair_rows[tile : tile + 1, :]).astype(F32).astype(BF16)
        )
    slab_high[...], slab_low[...] = split(inverse_ref[...])
    couple_high[...], couple_low[...] = split(coupling_ref[...])
    slab_map = (
        dot(slab_high[...], couple_high[...])
        + dot(slab_high[...], couple_low[...])
        + dot(slab_low[...], couple_high[...])
    )
    map_high[...], map_low[...] = split(slab_map)
    source = source_ref[...]
    base = product(jnp.broadcast_to(source, (16, orbitals)), slab_high[...], slab_low[...], NT)

    for load in loads:
        load.wait()
    scatter_wait(peers, me, first_send, first_recv, send_one, recv_one)

    blocks = first_recv[...].reshape(peers * 8, 128)
    low_lanes = lanes_of(blocks.shape) < 64
    high = blocks.astype(BF16).astype(F32)
    low = blocks - high
    stacked = jnp.concatenate(
        [
            jnp.where(low_lanes, high, roll(low, 64)).astype(BF16),
            jnp.where(low_lanes, roll(high, 64), low).astype(BF16),
        ],
        axis=0,
    )
    halves = dot(tables[0], stacked) + dot(tables[1], stacked)
    spectrum = halves + roll(halves, 64)
    spectrum_out[...] = spectrum
    other = roll(spectrum, 96)
    cos_a, sin_a, cos_b, sin_b = spectrum[:HALF], spectrum[HALF:], other[:HALF], other[HALF:]
    crossed = jnp.concatenate([cos_a * cos_b + sin_a * sin_b, sin_a * cos_b - cos_a * sin_b], axis=0)
    high = crossed.astype(BF16).astype(F32)
    packed = jnp.where(lanes_of(crossed.shape) < 32, high, roll(crossed - high, 32)).astype(BF16)
    halves = dot(inv_high[...], packed) + dot(inv_low[...], packed)
    polar = halves + roll(halves, 96)
    count = polar.shape[0] // 4
    group = lanes_of((count, 128)) // 32
    joined = polar[:count]
    for q in range(1, 4):
        joined = jnp.where(group == q, roll(polar[count * q : count * (q + 1)], 32 * q), joined)
    second_send[...] = joined.reshape(peers, 4, 128)
    scatter_start(peers, me, second_send, second_recv, send_two, recv_two)
    scatter_wait(peers, me, second_send, second_recv, send_two, recv_two)

    weighted = []
    for tile in range(8):
        lines = [second_recv[4 * tile + b] for b in range(4)]
        one, two = exchange_rows(jnp.concatenate(lines[:2], axis=0), jnp.concatenate(lines[2:], axis=0))
        weighted.append(jnp.concatenate([one, two], axis=0) * weight_ref[tile : tile + 1, :])
    both = dot(jnp.concatenate(split(jnp.concatenate(weighted, axis=1)), axis=0), orbital_table[...], NT)
    local_pol = both[:16] + both[16:]
    guess = base + product(local_pol * base, slab_high[...], slab_low[...], NT)
    upward[...] = product(guess, couple_high[...], couple_low[...], NN)

    upper[...] = jnp.zeros_like(upper)
    shift = pltpu.make_async_remote_copy(
        src_ref=upward,
        dst_ref=carried_in.at[0],
        send_sem=shift_sem.at[0],
        recv_sem=shift_sem.at[1],
        device_id={"section": before},
        device_id_type=MESH,
    )
    sweep = pltpu.make_async_remote_copy(
        src_ref=carried_out,
        dst_ref=carried_in.at[1],
        send_sem=sweep_sem.at[0],
        recv_sem=sweep_sem.at[1],
        device_id={"section": after},
        device_id_type=MESH,
    )

    @pl.when(has_before)
    def _():
        shift.start()

    partial = source + local_pol * guess

    @pl.when(has_after)
    def _():
        shift.wait_recv()
        upper[...] = carried_in[0]

    offset = product(partial + upper[...], slab_high[...], slab_low[...], NT)
    carried_out[...] = offset

    @pl.when(has_before)
    def _():
        sweep.wait_recv()
        carried_out[...] = offset + product(carried_in[1], map_high[...], map_low[...], NT)

    @pl.when(has_after)
    def _():
        sweep.start()

    screened = carried_out[...]
    both = dot(jnp.concatenate(split(screened), axis=0), orbital_table[...])
    pairs = both[:16] + both[16:]
    for tile in range(8):
        piece = pairs[:, 128 * tile : 128 * tile + 128] * weight_ref[tile : tile + 1, :]
        one, two = exchange_rows(piece[:8], piece[8:])
        for b, block in enumerate((one[:4], one[4:], two[:4], two[4:])):
            third_send[4 * tile + b] = block
    scatter_start(peers, me, third_send, values_out, send_three, recv_three)

    @pl.when(has_before)
    def _():
        shift.wait_send()

    @pl.when(has_after)
    def _():
        sweep.wait_send()

    scatter_wait(peers, me, third_send, values_out, send_three, recv_three)


def last_kernel(values_ref, spectrum_ref, fwd_high, fwd_low, inv_high, inv_low, sigma_ref):
    values = values_ref[...].reshape(values_ref.shape[0] * 4, 128)
    lane = lanes_of(values.shape)
    high = values.astype(BF16).astype(F32)
    low = values - high
    stacked = []
    for q in range(4):
        left = high if q == 0 else roll(high, 128 - 32 * q)
        right = roll(low, (160 - 32 * q) % 128) if q != 1 else low
        stacked.append(jnp.where(lane < 32, left, right).astype(BF16))
    stacked = jnp.concatenate(stacked, axis=0)
    halves = dot(fwd_high[...], stacked) + dot(fwd_low[...], stacked)
    wave = halves + roll(halves, 96)
    spectrum = spectrum_ref[...]
    cos_a, sin_a, cos_w, sin_w = spectrum[:HALF], spectrum[HALF:], wave[:HALF], wave[HALF:]
    crossed = jnp.concatenate([cos_a * cos_w - sin_a * sin_w, cos_a * sin_w + sin_a * cos_w], axis=0)
    high = crossed.astype(BF16).astype(F32)
    packed = jnp.where(lanes_of(crossed.shape) < 32, high, roll(crossed - high, 32)).astype(BF16)
    halves = dot(inv_high[...], packed) + dot(inv_low[...], packed)
    full = halves + roll(halves, 96)
    sigma_ref[...] = jnp.transpose(full)[:32]


def on_device(peers, sections, g_less, g_greater, partner, pair_rows, pair_weight, source, slab_inverse, coupling):
    own, _, columns = g_less.shape
    energies = own * peers
    orbitals = slab_inverse.shape[-1]
    polar_times = energy_order(peers, own, 4) - energies // 2
    sigma_times = np.arange(energies) + energies // 2
    vmem = pl.BlockSpec(memory_space=pltpu.VMEM)
    hbm = pl.BlockSpec(memory_space=pl.ANY)
    square = (orbitals, orbitals)
    strip = (own, orbitals)
    values, spectrum = pl.pallas_call(
        functools.partial(main_kernel, peers, sections),
        out_shape=(
            jax.ShapeDtypeStruct((peers, 4, 128), F32),
            jax.ShapeDtypeStruct((LENGTH, 128), F32),
        ),
        in_specs=[vmem] * 8 + [hbm] * 2 + [vmem] * 2,
        out_specs=(vmem, vmem),
        scratch_shapes=[
            pltpu.VMEM((128, 128), F32),
            pltpu.VMEM((peers, 8, 128), F32),
            pltpu.VMEM((peers, 8, 128), F32),
            pltpu.VMEM((peers, 4, 128), F32),
            pltpu.VMEM((peers, 4, 128), F32),
            pltpu.VMEM((peers, 4, 128), F32),
            pltpu.VMEM((2, LENGTH, energies), BF16),
            pltpu.SemaphoreType.DMA((2,)),
            pltpu.VMEM((orbitals, columns), BF16),
            pltpu.VMEM(square, BF16),
            pltpu.VMEM(square, BF16),
            pltpu.VMEM(square, BF16),
            pltpu.VMEM(square, BF16),
            pltpu.VMEM(square, BF16),
            pltpu.VMEM(square, BF16),
            pltpu.VMEM(strip, F32),
            pltpu.VMEM(strip, F32),
            pltpu.VMEM(strip, F32),
            pltpu.VMEM((2,) + strip, F32),
            pltpu.SemaphoreType.DMA((peers,)),
            pltpu.SemaphoreType.DMA((peers,)),
            pltpu.SemaphoreType.DMA((peers,)),
            pltpu.SemaphoreType.DMA((peers,)),
            pltpu.SemaphoreType.DMA((peers,)),
            pltpu.SemaphoreType.DMA((peers,)),
            pltpu.SemaphoreType.DMA((2,)),
            pltpu.SemaphoreType.DMA((2,)),
        ],
        compiler_params=pltpu.CompilerParams(
            collective_id=0, has_side_effects=True, vmem_limit_bytes=32 * 1024 * 1024
        ),
        name="update",
    )(
        g_less.reshape(-1, 128),
        g_greater.reshape(-1, 128),
        partner.reshape(-1, 128),
        pair_rows.reshape(-1, 128),
        pair_weight.reshape(-1, 128),
        source,
        slab_inverse[0],
        coupling[0],
        *forward_table(energy_order(peers, own, 2)),
        *inverse_table(polar_times, energies),
    )
    sigma = pl.pallas_call(
        last_kernel,
        out_shape=jax.ShapeDtypeStruct((columns // peers, energies), F32),
        in_specs=[vmem] * 6,
        out_specs=vmem,
        compiler_params=pltpu.CompilerParams(vmem_limit_bytes=32 * 1024 * 1024),
        name="convolution",
    )(
        values,
        spectrum,
        *forward_table(energy_order(peers, own, 4)),
        *inverse_table(sigma_times, energies),
    )
    return jnp.transpose(sigma)[:, None, :]


def solution(mesh):
    return jax.shard_map(
        functools.partial(on_device, mesh.shape["energy"], mesh.shape["section"]),
        mesh=mesh,
        in_specs=(
            P("energy", "section", None),
            P("energy", "section", None),
            P("section", None),
            P("section", None),
            P("section", None),
            P("section", None),
            P("section", None, None),
            P("section", None, None),
        ),
        out_specs=P(None, "section", "energy"),
        check_vma=False,
    )
```

profile of v0, /device:TPU:31, one launch (start us, length us, event | category | flops | bytes accessed | tf_op | source)
XLA Modules:
  0.0 111.1 jit_solution(16838142153512084570)
XLA Ops:
  0.0 0.0 copy-start.14
  0.0 0.0 copy-start.13
  0.0 0.0 copy-start.12
  0.0 0.7 copy-done.14
  0.7 0.0 copy-done.13
  0.7 0.0 copy-done.12
  0.7 0.0 copy-start
  0.7 1.2 %copy-done = f32[1,416,416]{2,1,0:T(8,128)S(1)} copy-done((f32[1,416,416]{2,1,0:T(8,128)S(1)}, f32[1,416,416]{2,1,0:T(8,128)}, u32[]{:S(2)}) %copy-start) | copy-done | bytes 692248
  1.9 0.0 copy-start.1
  1.9 1.2 %copy-done.1 = f32[1,416,416]{2,1,0:T(8,128)S(1)} copy-done((f32[1,416,416]{2,1,0:T(8,128)S(1)}, f32[1,416,416]{2,1,0:T(8,128)}, u32[]{:S(2)}) %copy-start.1) | copy-done | bytes 692248
  3.0 0.0 copy-start.6
  3.0 1.1 %copy-done.6 = bf16[512,768]{1,0:T(8,128)(2,1)S(1)} copy-done((bf16[512,768]{1,0:T(8,128)(2,1)S(1)}, bf16[512,768]{1,0:T(8,128)(2,1)}, u32[]{:S(2)}) %copy-start.6) | copy-done | bytes 786456
  4.2 0.0 copy-start.7
  4.2 1.1 %copy-done.7 = bf16[512,768]{1,0:T(8,128)(2,1)S(1)} copy-done((bf16[512,768]{1,0:T(8,128)(2,1)S(1)}, bf16[512,768]{1,0:T(8,128)(2,1)}, u32[]{:S(2)}) %copy-start.7) | copy-done | bytes 786456
  5.3 0.0 copy-start.8
  5.3 1.1 %copy-done.8 = bf16[768,512]{1,0:T(8,128)(2,1)S(1)} copy-done((bf16[768,512]{1,0:T(8,128)(2,1)S(1)}, bf16[768,512]{1,0:T(8,128)(2,1)}, u32[]{:S(2)}) %copy-start.8) | copy-done | bytes 786456
  6.4 0.0 copy-start.9
  6.4 1.1 %copy-done.9 = bf16[768,512]{1,0:T(8,128)(2,1)S(1)} copy-done((bf16[768,512]{1,0:T(8,128)(2,1)S(1)}, bf16[768,512]{1,0:T(8,128)(2,1)}, u32[]{:S(2)}) %copy-start.9) | copy-done | bytes 786456
  7.6 0.0 copy-start.10
  7.6 0.8 copy-done.10
  8.4 0.0 copy-start.11
  8.4 0.8 copy-done.11
  9.2 0.0 copy-start.15
  9.2 0.7 copy-done.15
  9.9 0.0 copy-start.3
  9.9 0.0 copy-start.4
  9.9 98.3 %update.1 = (f32[32,4,128]{2,1,0:T(4,128)S(1)}, f32[768,128]{1,0:T(8,128)S(1)}) custom-call(f32[128,128]{1,0:T(8,128)S(1)} %bitcast.12, f32[128,128]{1,0:T(8,128)S(1)} %bitcast.13, s32[8,128]{1,0:T(8,128)S(1)} %bitcast.14, s32[8,128]{1,0:T(8,128)S(1)} %bitcast.15, f32[8,128]{1,0:T(8,128)S(1)} %bitcast.16, f32[1,416]{1,0:T(1,128)S(1)} %copy-done.15, ...), custom_call_target="tpu_custom_call" | custom-call | tf_op jit(solution)/shard_map/update/pallas_call | solution.py:356
  108.2 0.0 copy-done.2
  108.2 0.0 copy-done.3
  108.2 0.0 copy-done.4
  108.3 0.0 copy-done.5
  108.3 2.9 %convolution.1 = f32[32,512]{1,0:T(8,128)} custom-call(f32[32,4,128]{2,1,0:T(4,128)S(1)} %get-tuple-element.7.values_ref, f32[768,128]{1,0:T(8,128)S(1)} %get-tuple-element.8.spectrum_ref, bf16[768,512]{1,0:T(8,128)(2,1)S(1)} %copy-done.5, bf16[768,512]{1,0:T(8,128)(2,1)S(1)} %copy-done.4, bf16[512,768]{1,0:T(8,128)(2,1)S(1)} %copy-done.3, ...), custom_call_target="tpu_custom_call" | custom-call | tf_op jit(solution)/shard_map/convolution/pallas_call | solution.py:409
  (2 shorter events, 0.0 us)
Async XLA Ops:
  0.0 0.7 copy-start.14
  0.0 0.7 copy-start.13
  0.0 0.7 copy-start.12
  0.7 1.2 %copy-start = (f32[1,416,416]{2,1,0:T(8,128)S(1)}, f32[1,416,416]{2,1,0:T(8,128)}, u32[]{:S(2)}) copy-start(f32[1,416,416]{2,1,0:T(8,128)} %param.22) | copy-start | bytes 2076676
  1.9 1.2 %copy-start.1 = (f32[1,416,416]{2,1,0:T(8,128)S(1)}, f32[1,416,416]{2,1,0:T(8,128)}, u32[]{:S(2)}) copy-start(f32[1,416,416]{2,1,0:T(8,128)} %param.23) | copy-start | bytes 2076676
  3.0 1.1 %copy-start.6 = (bf16[512,768]{1,0:T(8,128)(2,1)S(1)}, bf16[512,768]{1,0:T(8,128)(2,1)}, u32[]{:S(2)}) copy-start(bf16[512,768]{1,0:T(8,128)(2,1)} %constant.19.clone.inv_low) | copy-start | bytes 2359300
  4.2 1.1 %copy-start.7 = (bf16[512,768]{1,0:T(8,128)(2,1)S(1)}, bf16[512,768]{1,0:T(8,128)(2,1)}, u32[]{:S(2)}) copy-start(bf16[512,768]{1,0:T(8,128)(2,1)} %constant.18.clone.inv_high) | copy-start | bytes 2359300
  5.3 1.1 %copy-start.8 = (bf16[768,512]{1,0:T(8,128)(2,1)S(1)}, bf16[768,512]{1,0:T(8,128)(2,1)}, u32[]{:S(2)}) copy-start(bf16[768,512]{1,0:T(8,128)(2,1)} %constant.17.clone.fwd_low) | copy-start | bytes 2359300
  6.4 1.1 %copy-start.9 = (bf16[768,512]{1,0:T(8,128)(2,1)S(1)}, bf16[768,512]{1,0:T(8,128)(2,1)}, u32[]{:S(2)}) copy-start(bf16[768,512]{1,0:T(8,128)(2,1)} %constant.16.clone.fwd_high) | copy-start | bytes 2359300
  7.6 0.8 copy-start.10
  8.4 0.8 copy-start.11
  9.2 0.7 copy-start.15
  9.9 98.3 %copy-start.2 = (bf16[512,768]{1,0:T(8,128)(2,1)S(1)}, bf16[512,768]{1,0:T(8,128)(2,1)}, u32[]{:S(2)}) copy-start(bf16[512,768]{1,0:T(8,128)(2,1)} %constant.23.clone.inv_low) | copy-start | bytes 2359300
  9.9 98.3 %copy-start.3 = (bf16[512,768]{1,0:T(8,128)(2,1)S(1)}, bf16[512,768]{1,0:T(8,128)(2,1)}, u32[]{:S(2)}) copy-start(bf16[512,768]{1,0:T(8,128)(2,1)} %constant.22.clone.inv_high) | copy-start | bytes 2359300
  9.9 98.3 %copy-start.4 = (bf16[768,512]{1,0:T(8,128)(2,1)S(1)}, bf16[768,512]{1,0:T(8,128)(2,1)}, u32[]{:S(2)}) copy-start(bf16[768,512]{1,0:T(8,128)(2,1)} %constant.21.clone.fwd_low) | copy-start | bytes 2359300
  9.9 98.3 %copy-start.5 = (bf16[768,512]{1,0:T(8,128)(2,1)S(1)}, bf16[768,512]{1,0:T(8,128)(2,1)}, u32[]{:S(2)}) copy-start(bf16[768,512]{1,0:T(8,128)(2,1)} %constant.20.clone.fwd_high) | copy-start | bytes 2359300
where the time goes:
time: 112 us; the launch traced here: 111 us
  Pallas kernels  101 us (90%)
  local copies, waits for them, and re-layouts  9.93 us (9%)
    pallas_call x1, Pallas kernels, on_device(): pl.pallas_call(functools.partial(main_kernel, peers, sections), out_shape...  98.3 us
    unnamed x32, local copies, waits for them, and re-layouts  9.93 us
    pallas_call x1, Pallas kernels, on_device(): pl.pallas_call(last_kernel, out_shape=jax.ShapeDtypeStruct((columns // pe...  2.88 us

commit v1 on v0

--- a/solution.py
+++ b/solution.py
@@ -16,6 +16,7 @@
 NN = (((1,), (0,)), ((), ()))
 LENGTH = 768
 HALF = LENGTH // 2
+REACH = 4
 
 
 def two_parts(table):
@@ -98,38 +99,26 @@
 
 
 def scatter_start(peers, me, source, target, send, recv):
-    def one(k, _):
-        peer = lax.rem(me + k, peers)
+    def one(n, _):
+        away = peers // 2 + (n + 1) // 2 * (1 - n % 2 * 2)
+        peer = lax.rem(me + away, peers)
         pltpu.make_async_remote_copy(
             src_ref=source.at[peer],
             dst_ref=target.at[me],
-            send_sem=send.at[k],
-            recv_sem=recv.at[k],
+            send_sem=send,
+            recv_sem=recv,
             device_id={"energy": peer},
             device_id_type=MESH,
         ).start()
         return 0
 
-    lax.fori_loop(1, peers, one, 0)
+    lax.fori_loop(0, peers - 1, one, 0)
     target[me] = source[me]
 
 
-def scatter_wait(peers, me, source, target, send, recv):
-    def one(k, _):
-        peer = lax.rem(me + k, peers)
-        copy = pltpu.make_async_remote_copy(
-            src_ref=source.at[peer],
-            dst_ref=target.at[me],
-            send_sem=send.at[k],
-            recv_sem=recv.at[k],
-            device_id={"energy": peer},
-            device_id_type=MESH,
-        )
-        copy.wait_send()
-        copy.wait_recv()
-        return 0
-
-    lax.fori_loop(1, peers, one, 0)
+def wait_blocks(peers, ref, semaphore):
+    part = ref.at[pl.ds(0, peers - 1)]
+    pltpu.make_async_copy(part, part, semaphore).wait()
 
 
 def lane_take(x, index):
@@ -138,21 +127,38 @@
 
 def main_kernel(
     peers, sections,
+    less_hbm, great_hbm, partner_hbm, rows_hbm, weight_hbm, source_hbm, inverse_hbm, coupling_hbm,
+    fwd_high_hbm, fwd_low_hbm, inv_high_hbm, inv_low_hbm,
+    values_out, spectrum_out,
     less_ref, great_ref, partner_ref, rows_ref, weight_ref, source_ref, inverse_ref, coupling_ref,
-    fwd_high, fwd_low, inv_high, inv_low,
-    values_out, spectrum_out,
+    fwd_high, fwd_low, inv_high, inv_low, load_sem,
     swapped, first_send, first_recv, second_send, second_recv, third_send,
-    tables, table_sem, orbital_table, slab_high, slab_low, couple_high, couple_low, map_high, map_low,
-    upward, upper, carried_out, carried_in,
-    send_one, recv_one, send_two, recv_two, send_three, recv_three, shift_sem, sweep_sem,
+    orbital_table, slab_high, slab_low, couple_high, couple_low,
+    steps, inbox, step_high, step_low, next_send, next_recv, twin_send, twin_recv,
+    upward, offset, carried, arrived, across_send, across_recv,
+    send_one, recv_one, send_two, recv_two, send_three, recv_three,
 ):
     me = lax.axis_index("energy")
     section = lax.axis_index("section")
     has_before = section > 0
     has_after = section < sections - 1
-    before = lax.rem(section + sections - 1, sections)
     after = lax.rem(section + 1, sections)
     orbitals = inverse_ref.shape[0]
+    half, first_rows = orbitals // 2, orbitals // 64 * 16 + 16
+    core = lax.rem(me, 2)
+    twin = me + 1 - 2 * core
+
+    loads = [
+        pltpu.make_async_copy(source, target, load_sem.at[place])
+        for place, (source, target) in enumerate((
+            (great_hbm, great_ref), (partner_hbm, partner_ref), (less_hbm, less_ref), (rows_hbm, rows_ref),
+            (weight_hbm, weight_ref), (source_hbm, source_ref), (inverse_hbm, inverse_ref),
+            (coupling_hbm, coupling_ref), (fwd_high_hbm, fwd_high), (fwd_low_hbm, fwd_low),
+            (inv_high_hbm, inv_high), (inv_low_hbm, inv_low),
+        ))
+    ]
+    for load in loads:
+        load.start()
 
     barrier = pltpu.get_barrier_semaphore()
 
@@ -162,20 +168,16 @@
 
     lax.fori_loop(1, peers, greet, 0)
 
-    @pl.when(has_before)
-    def _():
-        pl.semaphore_signal(barrier, inc=1, device_id={"section": before}, device_id_type=MESH)
-
-    @pl.when(has_after)
-    def _():
-        pl.semaphore_signal(barrier, inc=1, device_id={"section": after}, device_id_type=MESH)
-
-    loads = [
-        pltpu.make_async_copy(ref, tables.at[place], table_sem.at[place])
-        for place, ref in enumerate((fwd_high, fwd_low))
-    ]
-    for load in loads:
-        load.start()
+    for away in range(1, REACH + 1):
+        for there, other in ((section >= away, section - away), (section < sections - away, section + away)):
+
+            @pl.when(there)
+            def _(other=other):
+                pl.semaphore_signal(barrier, inc=1, device_id={"section": other}, device_id_type=MESH)
+
+    loads[0].wait()
+    loads[1].wait()
+    loads[2].wait()
 
     partner = partner_ref[...]
     partner_tile, partner_lane = partner // 128, partner % 128
@@ -194,15 +196,63 @@
         for b, part in enumerate(exchange_groups(parts)):
             first_send[4 * tile + b] = part
 
-    pl.semaphore_wait(barrier, peers - 1 + has_before.astype(jnp.int32) + has_after.astype(jnp.int32))
+    pl.semaphore_wait(barrier, peers - 1 + jnp.minimum(section, REACH) + jnp.minimum(sections - 1 - section, REACH))
     scatter_start(peers, me, first_send, first_recv, send_one, recv_one)
 
-    pair_rows = rows_ref[...]
-    for tile in range(8):
-        index = lax.broadcasted_iota(jnp.int32, (orbitals, 128), 0)
-        orbital_table[:, 128 * tile : 128 * tile + 128] = (
-            (index == pair_rows[tile : tile + 1, :]).astype(F32).astype(BF16)
+    def rows_of(chunk):
+        return pl.ds(0, first_rows) if chunk == 0 else pl.ds(first_rows, half - first_rows)
+
+    def to_next(k, chunk):
+        return pltpu.make_async_remote_copy(
+            src_ref=steps.at[k - 1, core, rows_of(chunk)],
+            dst_ref=inbox.at[k - 1, rows_of(chunk)],
+            send_sem=next_send.at[k - 1, chunk],
+            recv_sem=next_recv.at[k - 1, chunk],
+            device_id={"section": after},
+            device_id_type=MESH,
         )
+
+    def to_twin(k, chunk):
+        return pltpu.make_async_remote_copy(
+            src_ref=steps.at[k - 1, core, rows_of(chunk)],
+            dst_ref=steps.at[k - 1, core, rows_of(chunk)],
+            send_sem=twin_send.at[k - 1, chunk],
+            recv_sem=twin_recv.at[k - 1, chunk],
+            device_id={"energy": twin},
+            device_id_type=MESH,
+        )
+
+    def pass_on(k, chunk):
+        @pl.when(has_after)
+        def _():
+            to_next(k, chunk).start()
+
+    def grow(k, chunk):
+        @pl.when(has_before)
+        def _():
+            to_next(k - 1, chunk).wait_recv()
+
+        rows = rows_of(chunk)
+        high, low = split(inbox[k - 2, rows])
+        whole_high, whole_low = step_high[0], step_low[0]
+        steps[k - 1, core, rows] = dot(high, whole_high) + dot(low, whole_high) + dot(high, whole_low)
+        if k < REACH:
+            pass_on(k, chunk)
+        to_twin(k, chunk).start()
+
+    def gather(k):
+        for chunk in range(2):
+            to_twin(k, chunk).wait_recv()
+        for part in range(2):
+            rows = pl.ds(half * part, half)
+            step_high[k - 1, rows], step_low[k - 1, rows] = split(steps[k - 1, part])
+
+    @pl.when(jnp.logical_not(has_before))
+    def _():
+        inbox[...] = jnp.zeros_like(inbox)
+
+    for load in loads[3:8]:
+        load.wait()
     slab_high[...], slab_low[...] = split(inverse_ref[...])
     couple_high[...], couple_low[...] = split(coupling_ref[...])
     slab_map = (
@@ -210,13 +260,29 @@
         + dot(slab_high[...], couple_low[...])
         + dot(slab_low[...], couple_high[...])
     )
-    map_high[...], map_low[...] = split(slab_map)
+    map_high, map_low = split(slab_map)
+    index = lax.broadcasted_iota(jnp.int32, (orbitals, orbitals), 0)
+    identity = (index == lanes_of((orbitals, orbitals))).astype(F32).astype(BF16)
+    turned_high, turned_low = dot(identity, map_high, NT), dot(identity, map_low, NT)
+    step_high[0], step_low[0] = turned_high.astype(BF16), turned_low.astype(BF16)
+    turned = turned_high + turned_low
+    steps[0, 0], steps[0, 1] = turned[:half], turned[half:]
+    for chunk in range(2):
+        pass_on(1, chunk)
+
+    pair_rows = rows_ref[...]
+    for tile in range(8):
+        index = lax.broadcasted_iota(jnp.int32, (orbitals, 128), 0)
+        orbital_table[:, 128 * tile : 128 * tile + 128] = (
+            (index == pair_rows[tile : tile + 1, :]).astype(F32).astype(BF16)
+        )
     source = source_ref[...]
     base = product(jnp.broadcast_to(source, (16, orbitals)), slab_high[...], slab_low[...], NT)
-
-    for load in loads:
+    grow(2, 0)
+
+    for load in loads[8:]:
         load.wait()
-    scatter_wait(peers, me, first_send, first_recv, send_one, recv_one)
+    wait_blocks(peers, first_recv, recv_one)
 
     blocks = first_recv[...].reshape(peers * 8, 128)
     low_lanes = lanes_of(blocks.shape) < 64
@@ -229,7 +295,7 @@
         ],
         axis=0,
     )
-    halves = dot(tables[0], stacked) + dot(tables[1], stacked)
+    halves = dot(fwd_high[...], stacked) + dot(fwd_low[...], stacked)
     spectrum = halves + roll(halves, 64)
     spectrum_out[...] = spectrum
     other = roll(spectrum, 96)
@@ -246,7 +312,10 @@
         joined = jnp.where(group == q, roll(polar[count * q : count * (q + 1)], 32 * q), joined)
     second_send[...] = joined.reshape(peers, 4, 128)
     scatter_start(peers, me, second_send, second_recv, send_two, recv_two)
-    scatter_wait(peers, me, second_send, second_recv, send_two, recv_two)
+    grow(2, 1)
+    grow(3, 0)
+    gather(2)
+    wait_blocks(peers, second_recv, recv_two)
 
     weighted = []
     for tile in range(8):
@@ -258,48 +327,69 @@
     guess = base + product(local_pol * base, slab_high[...], slab_low[...], NT)
     upward[...] = product(guess, couple_high[...], couple_low[...], NN)
 
-    upper[...] = jnp.zeros_like(upper)
-    shift = pltpu.make_async_remote_copy(
-        src_ref=upward,
-        dst_ref=carried_in.at[0],
-        send_sem=shift_sem.at[0],
-        recv_sem=shift_sem.at[1],
-        device_id={"section": before},
-        device_id_type=MESH,
-    )
-    sweep = pltpu.make_async_remote_copy(
-        src_ref=carried_out,
-        dst_ref=carried_in.at[1],
-        send_sem=sweep_sem.at[0],
-        recv_sem=sweep_sem.at[1],
-        device_id={"section": after},
-        device_id_type=MESH,
-    )
+    def across(source, place, away):
+        return pltpu.make_async_remote_copy(
+            src_ref=source,
+            dst_ref=arrived.at[place],
+            send_sem=across_send.at[place],
+            recv_sem=across_recv.at[place],
+            device_id={"section": lax.rem(section + sections + away, sections)},
+            device_id_type=MESH,
+        )
+
+    shift = across(upward, 0, -1)
+    window = [across(offset, away, away) for away in range(1, REACH)]
+    sweep = across(carried, REACH, REACH)
 
     @pl.when(has_before)
     def _():
         shift.start()
 
+    grow(3, 1)
     partial = source + local_pol * guess
 
     @pl.when(has_after)
     def _():
         shift.wait_recv()
-        upper[...] = carried_in[0]
-
-    offset = product(partial + upper[...], slab_high[...], slab_low[...], NT)
-    carried_out[...] = offset
-
-    @pl.when(has_before)
+
+    @pl.when(jnp.logical_not(has_after))
+    def _():
+        arrived[0] = jnp.zeros_like(upward)
+
+    offset[...] = product(partial + arrived[0], slab_high[...], slab_low[...], NT)
+    for away in range(1, REACH):
+
+        @pl.when(section < sections - away)
+        def _(away=away):
+            window[away - 1].start()
+
+    gather(3)
+    grow(4, 0)
+    carried[...] = offset[...]
+    for away in range(1, REACH):
+
+        @pl.when(section >= away)
+        def _(away=away):
+            window[away - 1].wait_recv()
+            carried[...] += product(arrived[away], step_high[away - 1], step_low[away - 1], NN)
+
+    @pl.when(section < REACH)
+    def _():
+        sweep.start()
+
+    grow(4, 1)
+    gather(4)
+
+    @pl.when(section >= REACH)
     def _():
         sweep.wait_recv()
-        carried_out[...] = offset + product(carried_in[1], map_high[...], map_low[...], NT)
-
-    @pl.when(has_after)
-    def _():
-        sweep.start()
-
-    screened = carried_out[...]
+        carried[...] += product(arrived[REACH], step_high[REACH - 1], step_low[REACH - 1], NN)
+
+        @pl.when(section < sections - REACH)
+        def _():
+            sweep.start()
+
+    screened = carried[...]
     both = dot(jnp.concatenate(split(screened), axis=0), orbital_table[...])
     pairs = both[:16] + both[16:]
     for tile in range(8):
@@ -313,11 +403,30 @@
     def _():
         shift.wait_send()
 
-    @pl.when(has_after)
+    for away in range(1, REACH):
+
+        @pl.when(section < sections - away)
+        def _(away=away):
+            window[away - 1].wait_send()
+
+    @pl.when(section < sections - REACH)
     def _():
         sweep.wait_send()
 
-    scatter_wait(peers, me, third_send, values_out, send_three, recv_three)
+    for chunk in range(2):
+
+        @pl.when(has_after)
+        def _(chunk=chunk):
+            for k in range(1, REACH):
+                to_next(k, chunk).wait_send()
+
+        for k in range(2, REACH + 1):
+            to_twin(k, chunk).wait_send()
+
+    wait_blocks(peers, first_send, send_one)
+    wait_blocks(peers, second_send, send_two)
+    wait_blocks(peers, third_send, send_three)
+    wait_blocks(peers, values_out, recv_three)
 
 
 def last_kernel(values_ref, spectrum_ref, fwd_high, fwd_low, inv_high, inv_low, sigma_ref):
@@ -350,7 +459,7 @@
     polar_times = energy_order(peers, own, 4) - energies // 2
     sigma_times = np.arange(energies) + energies // 2
     vmem = pl.BlockSpec(memory_space=pltpu.VMEM)
-    hbm = pl.BlockSpec(memory_space=pl.ANY)
+    hbm = pl.BlockSpec(memory_space=pltpu.HBM)
     square = (orbitals, orbitals)
     strip = (own, orbitals)
     values, spectrum = pl.pallas_call(
@@ -359,39 +468,51 @@
             jax.ShapeDtypeStruct((peers, 4, 128), F32),
             jax.ShapeDtypeStruct((LENGTH, 128), F32),
         ),
-        in_specs=[vmem] * 8 + [hbm] * 2 + [vmem] * 2,
+        in_specs=[hbm] * 12,
         out_specs=(vmem, vmem),
         scratch_shapes=[
+            pltpu.VMEM((128, 128), F32),
+            pltpu.VMEM((128, 128), F32),
+            pltpu.VMEM((8, 128), jnp.int32),
+            pltpu.VMEM((8, 128), jnp.int32),
+            pltpu.VMEM((8, 128), F32),
+            pltpu.VMEM((1, orbitals), F32),
+            pltpu.VMEM(square, F32),
+            pltpu.VMEM(square, F32),
+            pltpu.VMEM((LENGTH, energies), BF16),
+            pltpu.VMEM((LENGTH, energies), BF16),
+            pltpu.VMEM((energies, LENGTH), BF16),
+            pltpu.VMEM((energies, LENGTH), BF16),
+            pltpu.SemaphoreType.DMA((12,)),
             pltpu.VMEM((128, 128), F32),
             pltpu.VMEM((peers, 8, 128), F32),
             pltpu.VMEM((peers, 8, 128), F32),
             pltpu.VMEM((peers, 4, 128), F32),
             pltpu.VMEM((peers, 4, 128), F32),
             pltpu.VMEM((peers, 4, 128), F32),
-            pltpu.VMEM((2, LENGTH, energies), BF16),
-            pltpu.SemaphoreType.DMA((2,)),
             pltpu.VMEM((orbitals, columns), BF16),
             pltpu.VMEM(square, BF16),
             pltpu.VMEM(square, BF16),
             pltpu.VMEM(square, BF16),
             pltpu.VMEM(square, BF16),
-            pltpu.VMEM(square, BF16),
-            pltpu.VMEM(square, BF16),
+            pltpu.VMEM((REACH, 2, orbitals // 2, orbitals), F32),
+            pltpu.VMEM((REACH - 1, orbitals // 2, orbitals), F32),
+            pltpu.VMEM((REACH,) + square, BF16),
+            pltpu.VMEM((REACH,) + square, BF16),
+            pltpu.SemaphoreType.DMA((REACH, 2)),
+            pltpu.SemaphoreType.DMA((REACH, 2)),
+            pltpu.SemaphoreType.DMA((REACH, 2)),
+            pltpu.SemaphoreType.DMA((REACH, 2)),
             pltpu.VMEM(strip, F32),
             pltpu.VMEM(strip, F32),
             pltpu.VMEM(strip, F32),
-            pltpu.VMEM((2,) + strip, F32),
-            pltpu.SemaphoreType.DMA((peers,)),
-            pltpu.SemaphoreType.DMA((peers,)),
-            pltpu.SemaphoreType.DMA((peers,)),
-            pltpu.SemaphoreType.DMA((peers,)),
-            pltpu.SemaphoreType.DMA((peers,)),
-            pltpu.SemaphoreType.DMA((peers,)),
-            pltpu.SemaphoreType.DMA((2,)),
-            pltpu.SemaphoreType.DMA((2,)),
-        ],
+            pltpu.VMEM((REACH + 1,) + strip, F32),
+            pltpu.SemaphoreType.DMA((REACH + 1,)),
+            pltpu.SemaphoreType.DMA((REACH + 1,)),
+        ]
+        + [pltpu.SemaphoreType.DMA] * 6,
         compiler_params=pltpu.CompilerParams(
-            collective_id=0, has_side_effects=True, vmem_limit_bytes=32 * 1024 * 1024
+            collective_id=0, has_side_effects=True, vmem_limit_bytes=60 * 1024 * 1024
         ),
         name="update",
     )(

time: 112 us -> 70.2 us (0.63)
  the two profiles are of different devices: /device:TPU:31 before, /device:TPU:25 now
where the time goes in v1:
time: 70.2 us; the launch traced here: 70 us
  Pallas kernels  68.1 us (97%)
  local copies, waits for them, and re-layouts  1.85 us (3%)
    pallas_call x1, Pallas kernels, on_device(): pl.pallas_call(functools.partial(main_kernel, peers, sections), out_shape...  65.2 us
    pallas_call x1, Pallas kernels, on_device(): pl.pallas_call(last_kernel, out_shape=jax.ShapeDtypeStruct((columns // pe...  2.88 us
    unnamed x12, local copies, waits for them, and re-layouts  1.85 us

profile of v1, /device:TPU:25, one launch (start us, length us, event | category | flops | bytes accessed | tf_op | source)
XLA Modules:
  0.0 70.0 jit_solution(17376550147079743996)
XLA Ops:
  0.0 0.0 copy-start
  0.0 0.0 copy-start.1
  0.0 0.0 copy-start.2
  0.0 0.0 copy-start.3
  0.0 65.2 %update.1 = (f32[32,4,128]{2,1,0:T(4,128)}, f32[768,128]{1,0:T(8,128)}) custom-call(f32[128,128]{1,0:T(8,128)} %bitcast.12, f32[128,128]{1,0:T(8,128)} %bitcast.13, s32[8,128]{1,0:T(8,128)} %bitcast.14, s32[8,128]{1,0:T(8,128)} %bitcast.15, f32[8,128]{1,0:T(8,128)} %bitcast.16, f32[1,416]{1,0:T(1,128)} %source_hbm.1, f32[416,416]{1,0:T(8,128)} %bitcast.10, ...), custom_call_target="tpu_custom_call" | custom-call | tf_op jit(solution)/shard_map/update/pallas_call | solution.py:465
  65.3 0.0 copy-done
  65.3 0.0 copy-done.1
  65.3 0.0 copy-done.2
  65.3 0.0 copy-done.3
  65.3 0.0 copy-start.4
  65.3 1.0 %copy-done.4 = f32[768,128]{1,0:T(8,128)S(1)} copy-done((f32[768,128]{1,0:T(8,128)S(1)}, f32[768,128]{1,0:T(8,128)}, u32[]{:S(2)}) %copy-start.4) | copy-done | bytes 393240
  66.3 0.0 copy-start.5
  66.3 0.8 %copy-done.5 = f32[32,4,128]{2,1,0:T(4,128)S(1)} copy-done((f32[32,4,128]{2,1,0:T(4,128)S(1)}, f32[32,4,128]{2,1,0:T(4,128)}, u32[]{:S(2)}) %copy-start.5) | copy-done | bytes 65560
  67.1 2.9 %convolution.1 = f32[32,512]{1,0:T(8,128)} custom-call(f32[32,4,128]{2,1,0:T(4,128)S(1)} %copy-done.5, f32[768,128]{1,0:T(8,128)S(1)} %copy-done.4, bf16[768,512]{1,0:T(8,128)(2,1)S(1)} %copy-done.3, bf16[768,512]{1,0:T(8,128)(2,1)S(1)} %copy-done.2, bf16[512,768]{1,0:T(8,128)(2,1)S(1)} %copy-done.1, bf16[512,768]{1,0:T(8,128)(2,1)S(1)} %copy-done), custom_call_target="tpu_custom_call" | custom-call | tf_op jit(solution)/shard_map/convolution/pallas_call | solution.py:530
Async XLA Ops:
  0.0 65.3 %copy-start = (bf16[512,768]{1,0:T(8,128)(2,1)S(1)}, bf16[512,768]{1,0:T(8,128)(2,1)}, u32[]{:S(2)}) copy-start(bf16[512,768]{1,0:T(8,128)(2,1)} %constant.23.clone.inv_low) | copy-start | bytes 2359300
  0.0 65.3 %copy-start.1 = (bf16[512,768]{1,0:T(8,128)(2,1)S(1)}, bf16[512,768]{1,0:T(8,128)(2,1)}, u32[]{:S(2)}) copy-start(bf16[512,768]{1,0:T(8,128)(2,1)} %constant.22.clone.inv_high) | copy-start | bytes 2359300
  0.0 65.3 %copy-start.2 = (bf16[768,512]{1,0:T(8,128)(2,1)S(1)}, bf16[768,512]{1,0:T(8,128)(2,1)}, u32[]{:S(2)}) copy-start(bf16[768,512]{1,0:T(8,128)(2,1)} %constant.21.clone.fwd_low) | copy-start | bytes 2359300
  0.0 65.3 %copy-start.3 = (bf16[768,512]{1,0:T(8,128)(2,1)S(1)}, bf16[768,512]{1,0:T(8,128)(2,1)}, u32[]{:S(2)}) copy-start(bf16[768,512]{1,0:T(8,128)(2,1)} %constant.20.clone.fwd_high) | copy-start | bytes 2359300
  65.3 1.0 %copy-start.4 = (f32[768,128]{1,0:T(8,128)S(1)}, f32[768,128]{1,0:T(8,128)}, u32[]{:S(2)}) copy-start(f32[768,128]{1,0:T(8,128)} %get-tuple-element.8.spectrum_ref) | copy-start | bytes 1179652
  66.3 0.8 %copy-start.5 = (f32[32,4,128]{2,1,0:T(4,128)S(1)}, f32[32,4,128]{2,1,0:T(4,128)}, u32[]{:S(2)}) copy-start(f32[32,4,128]{2,1,0:T(4,128)} %get-tuple-element.7.values_ref) | copy-start | bytes 196612

commit v2 on v1

--- a/solution.py
+++ b/solution.py
@@ -98,10 +98,13 @@
     return both[:rows] + both[rows:] + dot(x_high, low, dims)
 
 
+def far_first(peers, n):
+    return peers // 2 + (n + 1) // 2 * (1 - n % 2 * 2)
+
+
 def scatter_start(peers, me, source, target, send, recv):
     def one(n, _):
-        away = peers // 2 + (n + 1) // 2 * (1 - n % 2 * 2)
-        peer = lax.rem(me + away, peers)
+        peer = lax.rem(me + far_first(peers, n), peers)
         pltpu.make_async_remote_copy(
             src_ref=source.at[peer],
             dst_ref=target.at[me],
@@ -121,6 +124,28 @@
     pltpu.make_async_copy(part, part, semaphore).wait()
 
 
+def chunk_rows(chunk):
+    return slice(0, 128) if chunk == 0 else slice(128, 208)
+
+
+def fold_rest(rows):
+    count, columns = rows.shape
+    tail = rows[:, columns // 128 * 128 :]
+    tail = jnp.concatenate([tail, jnp.zeros((count, 128 - tail.shape[1]), F32)], axis=1)
+    if count < 128:
+        tail = jnp.concatenate([tail, jnp.zeros((128 - count, 128), F32)], axis=0)
+    group = lanes_of((32, 128)) // 32
+    folded = tail[:32]
+    for g in range(1, 4):
+        folded = jnp.where(group == g, roll(tail[32 * g : 32 * g + 32], 32 * g), folded)
+    return folded
+
+
+def unfold_rest(folded, count):
+    groups = [folded] + [roll(folded, 128 - 32 * g) for g in range(1, 4)]
+    return jnp.concatenate(groups, axis=0)[:count, :32]
+
+
 def lane_take(x, index):
     return jnp.take_along_axis(x, index, axis=1, mode="promise_in_bounds")
 
@@ -134,7 +159,7 @@
     fwd_high, fwd_low, inv_high, inv_low, load_sem,
     swapped, first_send, first_recv, second_send, second_recv, third_send,
     orbital_table, slab_high, slab_low, couple_high, couple_low,
-    steps, inbox, step_high, step_low, next_send, next_recv, twin_send, twin_recv,
+    steps, inbox, rest, rest_in, step_high, step_low, next_send, next_recv, twin_send, twin_recv,
     upward, offset, carried, arrived, across_send, across_recv,
     send_one, recv_one, send_two, recv_two, send_three, recv_three,
 ):
@@ -144,7 +169,7 @@
     has_after = section < sections - 1
     after = lax.rem(section + 1, sections)
     orbitals = inverse_ref.shape[0]
-    half, first_rows = orbitals // 2, orbitals // 64 * 16 + 16
+    half, full = orbitals // 2, orbitals // 128 * 128
     core = lax.rem(me, 2)
     twin = me + 1 - 2 * core
 
@@ -162,11 +187,12 @@
 
     barrier = pltpu.get_barrier_semaphore()
 
-    def greet(k, _):
-        pl.semaphore_signal(barrier, inc=1, device_id={"energy": lax.rem(me + k, peers)}, device_id_type=MESH)
+    def greet(n, _):
+        peer = lax.rem(me + far_first(peers, n), peers)
+        pl.semaphore_signal(barrier, inc=1, device_id={"energy": peer}, device_id_type=MESH)
         return 0
 
-    lax.fori_loop(1, peers, greet, 0)
+    lax.fori_loop(0, peers - 1, greet, 0)
 
     for away in range(1, REACH + 1):
         for there, other in ((section >= away, section - away), (section < sections - away, section + away)):
@@ -195,61 +221,6 @@
                 parts.append(ref[pl.ds(64 * h + tile, 8, stride=8), :])
         for b, part in enumerate(exchange_groups(parts)):
             first_send[4 * tile + b] = part
-
-    pl.semaphore_wait(barrier, peers - 1 + jnp.minimum(section, REACH) + jnp.minimum(sections - 1 - section, REACH))
-    scatter_start(peers, me, first_send, first_recv, send_one, recv_one)
-
-    def rows_of(chunk):
-        return pl.ds(0, first_rows) if chunk == 0 else pl.ds(first_rows, half - first_rows)
-
-    def to_next(k, chunk):
-        return pltpu.make_async_remote_copy(
-            src_ref=steps.at[k - 1, core, rows_of(chunk)],
-            dst_ref=inbox.at[k - 1, rows_of(chunk)],
-            send_sem=next_send.at[k - 1, chunk],
-            recv_sem=next_recv.at[k - 1, chunk],
-            device_id={"section": after},
-            device_id_type=MESH,
-        )
-
-    def to_twin(k, chunk):
-        return pltpu.make_async_remote_copy(
-            src_ref=steps.at[k - 1, core, rows_of(chunk)],
-            dst_ref=steps.at[k - 1, core, rows_of(chunk)],
-            send_sem=twin_send.at[k - 1, chunk],
-            recv_sem=twin_recv.at[k - 1, chunk],
-            device_id={"energy": twin},
-            device_id_type=MESH,
-        )
-
-    def pass_on(k, chunk):
-        @pl.when(has_after)
-        def _():
-            to_next(k, chunk).start()
-
-    def grow(k, chunk):
-        @pl.when(has_before)
-        def _():
-            to_next(k - 1, chunk).wait_recv()
-
-        rows = rows_of(chunk)
-        high, low = split(inbox[k - 2, rows])
-        whole_high, whole_low = step_high[0], step_low[0]
-        steps[k - 1, core, rows] = dot(high, whole_high) + dot(low, whole_high) + dot(high, whole_low)
-        if k < REACH:
-            pass_on(k, chunk)
-        to_twin(k, chunk).start()
-
-    def gather(k):
-        for chunk in range(2):
-            to_twin(k, chunk).wait_recv()
-        for part in range(2):
-            rows = pl.ds(half * part, half)
-            step_high[k - 1, rows], step_low[k - 1, rows] = split(steps[k - 1, part])
-
-    @pl.when(jnp.logical_not(has_before))
-    def _():
-        inbox[...] = jnp.zeros_like(inbox)
 
     for load in loads[3:8]:
         load.wait()
@@ -267,6 +238,79 @@
     step_high[0], step_low[0] = turned_high.astype(BF16), turned_low.astype(BF16)
     turned = turned_high + turned_low
     steps[0, 0], steps[0, 1] = turned[:half], turned[half:]
+    own_half = steps[0, core]
+    for chunk in range(2):
+        rest[0, chunk] = fold_rest(own_half[chunk_rows(chunk)])
+
+    pl.semaphore_wait(barrier, peers - 1 + jnp.minimum(section, REACH) + jnp.minimum(sections - 1 - section, REACH))
+    scatter_start(peers, me, first_send, first_recv, send_one, recv_one)
+
+    def rows_of(chunk):
+        rows = chunk_rows(chunk)
+        return pl.ds(rows.start, rows.stop - rows.start)
+
+    def to_next(k, chunk):
+        def copy(source, target, place):
+            return pltpu.make_async_remote_copy(
+                src_ref=source,
+                dst_ref=target,
+                send_sem=next_send.at[k - 1, chunk, place],
+                recv_sem=next_recv.at[k - 1, chunk, place],
+                device_id={"section": after},
+                device_id_type=MESH,
+            )
+
+        whole = pl.ds(0, full)
+        return (
+            copy(steps.at[k - 1, core, rows_of(chunk), whole], inbox.at[k - 1, rows_of(chunk)], 0),
+            copy(rest.at[k - 1, chunk], rest_in.at[k - 1, chunk], 1),
+        )
+
+    def to_twin(k, chunk):
+        return pltpu.make_async_remote_copy(
+            src_ref=steps.at[k - 1, core, rows_of(chunk)],
+            dst_ref=steps.at[k - 1, core, rows_of(chunk)],
+            send_sem=twin_send.at[k - 1, chunk],
+            recv_sem=twin_recv.at[k - 1, chunk],
+            device_id={"energy": twin},
+            device_id_type=MESH,
+        )
+
+    def pass_on(k, chunk):
+        @pl.when(has_after)
+        def _():
+            for copy in to_next(k, chunk):
+                copy.start()
+
+    def grow(k, chunk):
+        @pl.when(has_before)
+        def _():
+            for copy in to_next(k - 1, chunk):
+                copy.wait_recv()
+
+        rows = rows_of(chunk)
+        last = unfold_rest(rest_in[k - 2, chunk], rows.size)
+        high, low = split(jnp.concatenate([inbox[k - 2, rows], last], axis=1))
+        whole_high, whole_low = step_high[0], step_low[0]
+        grown = dot(high, whole_high) + dot(low, whole_high) + dot(high, whole_low)
+        steps[k - 1, core, rows] = grown
+        if k < REACH:
+            rest[k - 1, chunk] = fold_rest(grown)
+            pass_on(k, chunk)
+        to_twin(k, chunk).start()
+
+    def gather(k):
+        for chunk in range(2):
+            to_twin(k, chunk).wait_recv()
+        for part in range(2):
+            rows = pl.ds(half * part, half)
+            step_high[k - 1, rows], step_low[k - 1, rows] = split(steps[k - 1, part])
+
+    @pl.when(jnp.logical_not(has_before))
+    def _():
+        inbox[...] = jnp.zeros_like(inbox)
+        rest_in[...] = jnp.zeros_like(rest_in)
+
     for chunk in range(2):
         pass_on(1, chunk)
 
@@ -315,6 +359,8 @@
     grow(2, 1)
     grow(3, 0)
     gather(2)
+    grow(3, 1)
+    gather(3)
     wait_blocks(peers, second_recv, recv_two)
 
     weighted = []
@@ -345,7 +391,7 @@
     def _():
         shift.start()
 
-    grow(3, 1)
+    grow(4, 0)
     partial = source + local_pol * guess
 
     @pl.when(has_after)
@@ -363,8 +409,8 @@
         def _(away=away):
             window[away - 1].start()
 
-    gather(3)
-    grow(4, 0)
+    grow(4, 1)
+    gather(4)
     carried[...] = offset[...]
     for away in range(1, REACH):
 
@@ -377,8 +423,6 @@
     def _():
         sweep.start()
 
-    grow(4, 1)
-    gather(4)
 
     @pl.when(section >= REACH)
     def _():
@@ -418,7 +462,8 @@
         @pl.when(has_after)
         def _(chunk=chunk):
             for k in range(1, REACH):
-                to_next(k, chunk).wait_send()
+                for copy in to_next(k, chunk):
+                    copy.wait_send()
 
         for k in range(2, REACH + 1):
             to_twin(k, chunk).wait_send()
@@ -496,11 +541,13 @@
             pltpu.VMEM(square, BF16),
             pltpu.VMEM(square, BF16),
             pltpu.VMEM((REACH, 2, orbitals // 2, orbitals), F32),
-            pltpu.VMEM((REACH - 1, orbitals // 2, orbitals), F32),
+            pltpu.VMEM((REACH - 1, orbitals // 2, orbitals // 128 * 128), F32),
+            pltpu.VMEM((REACH - 1, 2, 32, 128), F32),
+            pltpu.VMEM((REACH - 1, 2, 32, 128), F32),
             pltpu.VMEM((REACH,) + square, BF16),
             pltpu.VMEM((REACH,) + square, BF16),
-            pltpu.SemaphoreType.DMA((REACH, 2)),
-            pltpu.SemaphoreType.DMA((REACH, 2)),
+            pltpu.SemaphoreType.DMA((REACH, 2, 2)),
+            pltpu.SemaphoreType.DMA((REACH, 2, 2)),
             pltpu.SemaphoreType.DMA((REACH, 2)),
             pltpu.SemaphoreType.DMA((REACH, 2)),
             pltpu.VMEM(strip, F32),

time: 70.2 us -> 64.6 us (0.920)
  Pallas kernels: 68.1 us -> 62.6 us
    pallas_call x1, Pallas kernels: 65.2 us -> 59.7 us  [on_device(): pl.pallas_call(functools.partial(main_kernel, peers, sections), out_shape...]
where the time goes in v2:
time: 64.6 us; the launch traced here: 64.5 us
  Pallas kernels  62.6 us (97%)
  local copies, waits for them, and re-layouts  1.85 us (3%)
    pallas_call x1, Pallas kernels, on_device(): pl.pallas_call(functools.partial(main_kernel, peers, sections), out_shape...  59.7 us
    pallas_call x1, Pallas kernels, on_device(): pl.pallas_call(last_kernel, out_shape=jax.ShapeDtypeStruct((columns // pe...  2.88 us
    unnamed x12, local copies, waits for them, and re-layouts  1.85 us

profile of v2, /device:TPU:25, one launch (start us, length us, event | category | flops | bytes accessed | tf_op | source)
XLA Modules:
  0.0 64.5 jit_solution(13486135637988082719)
XLA Ops:
  0.0 0.0 copy-start
  0.0 0.0 copy-start.1
  0.0 0.0 copy-start.2
  0.0 0.0 copy-start.3
  0.0 59.7 %update.1 = (f32[32,4,128]{2,1,0:T(4,128)}, f32[768,128]{1,0:T(8,128)}) custom-call(f32[128,128]{1,0:T(8,128)} %bitcast.12, f32[128,128]{1,0:T(8,128)} %bitcast.13, s32[8,128]{1,0:T(8,128)} %bitcast.14, s32[8,128]{1,0:T(8,128)} %bitcast.15, f32[8,128]{1,0:T(8,128)} %bitcast.16, f32[1,416]{1,0:T(1,128)} %source_hbm.1, f32[416,416]{1,0:T(8,128)} %bitcast.10, ...), custom_call_target="tpu_custom_call" | custom-call | tf_op jit(solution)/shard_map/update/pallas_call | solution.py:510
  59.7 0.0 copy-done
  59.7 0.0 copy-done.1
  59.7 0.0 copy-done.2
  59.7 0.0 copy-done.3
  59.7 0.0 copy-start.4
  59.8 1.0 %copy-done.4 = f32[768,128]{1,0:T(8,128)S(1)} copy-done((f32[768,128]{1,0:T(8,128)S(1)}, f32[768,128]{1,0:T(8,128)}, u32[]{:S(2)}) %copy-start.4) | copy-done | bytes 393240
  60.7 0.0 copy-start.5
  60.7 0.8 %copy-done.5 = f32[32,4,128]{2,1,0:T(4,128)S(1)} copy-done((f32[32,4,128]{2,1,0:T(4,128)S(1)}, f32[32,4,128]{2,1,0:T(4,128)}, u32[]{:S(2)}) %copy-start.5) | copy-done | bytes 65560
  61.6 2.9 %convolution.1 = f32[32,512]{1,0:T(8,128)} custom-call(f32[32,4,128]{2,1,0:T(4,128)S(1)} %copy-done.5, f32[768,128]{1,0:T(8,128)S(1)} %copy-done.4, bf16[768,512]{1,0:T(8,128)(2,1)S(1)} %copy-done.3, bf16[768,512]{1,0:T(8,128)(2,1)S(1)} %copy-done.2, bf16[512,768]{1,0:T(8,128)(2,1)S(1)} %copy-done.1, bf16[512,768]{1,0:T(8,128)(2,1)S(1)} %copy-done), custom_call_target="tpu_custom_call" | custom-call | tf_op jit(solution)/shard_map/convolution/pallas_call | solution.py:577
Async XLA Ops:
  0.0 59.7 %copy-start = (bf16[512,768]{1,0:T(8,128)(2,1)S(1)}, bf16[512,768]{1,0:T(8,128)(2,1)}, u32[]{:S(2)}) copy-start(bf16[512,768]{1,0:T(8,128)(2,1)} %constant.23.clone.inv_low) | copy-start | bytes 2359300
  0.0 59.7 %copy-start.1 = (bf16[512,768]{1,0:T(8,128)(2,1)S(1)}, bf16[512,768]{1,0:T(8,128)(2,1)}, u32[]{:S(2)}) copy-start(bf16[512,768]{1,0:T(8,128)(2,1)} %constant.22.clone.inv_high) | copy-start | bytes 2359300
  0.0 59.7 %copy-start.2 = (bf16[768,512]{1,0:T(8,128)(2,1)S(1)}, bf16[768,512]{1,0:T(8,128)(2,1)}, u32[]{:S(2)}) copy-start(bf16[768,512]{1,0:T(8,128)(2,1)} %constant.21.clone.fwd_low) | copy-start | bytes 2359300
  0.0 59.7 %copy-start.3 = (bf16[768,512]{1,0:T(8,128)(2,1)S(1)}, bf16[768,512]{1,0:T(8,128)(2,1)}, u32[]{:S(2)}) copy-start(bf16[768,512]{1,0:T(8,128)(2,1)} %constant.20.clone.fwd_high) | copy-start | bytes 2359300
  59.7 1.0 %copy-start.4 = (f32[768,128]{1,0:T(8,128)S(1)}, f32[768,128]{1,0:T(8,128)}, u32[]{:S(2)}) copy-start(f32[768,128]{1,0:T(8,128)} %get-tuple-element.8.spectrum_ref) | copy-start | bytes 1179652
  60.7 0.8 %copy-start.5 = (f32[32,4,128]{2,1,0:T(4,128)S(1)}, f32[32,4,128]{2,1,0:T(4,128)}, u32[]{:S(2)}) copy-start(f32[32,4,128]{2,1,0:T(4,128)} %get-tuple-element.7.values_ref) | copy-start | bytes 196612

commit v3 on v2

--- a/solution.py
+++ b/solution.py
@@ -26,24 +26,31 @@
     return jnp.asarray(high), jnp.asarray(low)
 
 
-def angles(times):
-    return np.outer(np.arange(HALF) + 0.5, np.asarray(times, np.float64)) * (2.0 * math.pi / LENGTH)
-
-
-def forward_table(order):
-    phase = angles(order)
+def angles(order, energies):
+    times = np.asarray(order, np.float64) - (energies - 1) / 2
+    return np.outer(np.arange(HALF) + 0.5, times) * (2.0 * math.pi / LENGTH)
+
+
+def forward_table(order, energies):
+    phase = angles(order, energies)
     return two_parts(np.concatenate([np.cos(phase), np.sin(phase)], axis=0))
 
 
-def inverse_table(times, energies):
-    phase = angles(times).T
+def inverse_table(order, energies):
+    phase = angles(order, energies).T
     scale = 2.0 / LENGTH / math.sqrt(energies)
-    return two_parts(np.concatenate([np.cos(phase), np.sin(phase)], axis=1) * scale)
+    return two_parts(np.concatenate([np.cos(phase), np.sin(phase)], axis=0) * scale)
+
+
+def half_steps():
+    phase = (np.arange(HALF) + 0.5) * (math.pi / LENGTH)
+    table = np.concatenate([np.cos(phase), np.sin(phase)])
+    return jnp.asarray(np.broadcast_to(table[:, None], (LENGTH, 128)).astype(np.float32))
 
 
 def energy_order(peers, own, fold):
     rows = own // fold
-    group, sender, row = np.meshgrid(np.arange(fold), np.arange(peers), np.arange(rows), indexing="ij")
+    group, sender, row = np.meshgrid(np.arange(fold), np.arange(peers // 2), np.arange(rows), indexing="ij")
     return (sender * own + group * rows + row).reshape(-1)
 
 
@@ -102,12 +109,14 @@
     return peers // 2 + (n + 1) // 2 * (1 - n % 2 * 2)
 
 
-def scatter_start(peers, me, source, target, send, recv):
+def scatter_start(peers, me, source, target, send, recv, source_place, target_place):
+    mine = target_place(me)
+
     def one(n, _):
         peer = lax.rem(me + far_first(peers, n), peers)
         pltpu.make_async_remote_copy(
-            src_ref=source.at[peer],
-            dst_ref=target.at[me],
+            src_ref=source.at[source_place(peer)],
+            dst_ref=target.at[mine],
             send_sem=send,
             recv_sem=recv,
             device_id={"energy": peer},
@@ -116,7 +125,7 @@
         return 0
 
     lax.fori_loop(0, peers - 1, one, 0)
-    target[me] = source[me]
+    target[mine] = source[source_place(me)]
 
 
 def wait_blocks(peers, ref, semaphore):
@@ -146,19 +155,76 @@
     return jnp.concatenate(groups, axis=0)[:count, :32]
 
 
+def backward(inv_high, inv_low, real, turned):
+    def one(rows, x):
+        high = x.astype(BF16).astype(F32)
+        packed = jnp.where(lanes_of(x.shape) < 32, high, roll(x - high, 32)).astype(BF16)
+        halves = dot(inv_high[rows], packed) + dot(inv_low[rows], packed)
+        return halves + roll(halves, 96)
+
+    count = inv_high.shape[0] // 2
+    return one(pl.ds(0, count), real), one(pl.ds(count, count), turned)
+
+
 def lane_take(x, index):
     return jnp.take_along_axis(x, index, axis=1, mode="promise_in_bounds")
+
+
+def convolve(values_ref, spectrum_ref, fwd_high, fwd_low, inv_high, inv_low, half_step, sigma_ref):
+    senders = values_ref.shape[0] // 2
+    first = values_ref[:senders].reshape(senders * 4, 128)
+    second = values_ref[senders:].reshape(senders * 4, 128)
+    lane = lanes_of(first.shape)
+
+    def parts_of(x):
+        high = x.astype(BF16).astype(F32)
+        low = x - high
+        stacked = []
+        for q in range(4):
+            left = high if q == 0 else roll(high, 128 - 32 * q)
+            right = low if q == 1 else roll(low, (160 - 32 * q) % 128)
+            stacked.append(jnp.where(lane < 32, left, right))
+        return jnp.concatenate(stacked, axis=0).astype(BF16)
+
+    def forward(rows, x):
+        halves = dot(fwd_high[rows], x) + dot(fwd_low[rows], x)
+        return halves + roll(halves, 96)
+
+    cosines, sines = pl.ds(0, HALF), pl.ds(HALF, HALF)
+    cos_w, sin_w = forward(cosines, parts_of(first + second)), forward(sines, parts_of(first - second))
+    cos_a, sin_a = spectrum_ref[cosines], spectrum_ref[sines]
+    real, turned = cos_a * cos_w - sin_a * sin_w, cos_a * sin_w + sin_a * cos_w
+    cos_half, sin_half = half_step[cosines], half_step[sines]
+    even, odd = backward(
+        inv_high, inv_low, real * cos_half + turned * sin_half, turned * cos_half - real * sin_half
+    )
+    count = even.shape[0]
+    later = even - odd
+    lane = lanes_of(later.shape)
+    high = later.astype(BF16).astype(F32)
+    middle = (later - high).astype(BF16).astype(F32)
+    low = later - high - middle
+    packed = jnp.where(lane < 32, high, jnp.where(lane < 64, roll(middle, 32), roll(low, 64))).astype(BF16)
+    row = lax.broadcasted_iota(jnp.int32, (count, count), 0)
+    reverse = (row + lanes_of((count, count)) == count - 1).astype(F32).astype(BF16)
+    turned_round = dot(reverse, packed)
+    later = turned_round + roll(turned_round, 96) + roll(turned_round, 64)
+    sigma_ref[:, :count] = jnp.transpose(even + odd)[:32]
+    sigma_ref[:, count:] = jnp.transpose(later)[:32]
 
 
 def main_kernel(
     peers, sections,
     less_hbm, great_hbm, partner_hbm, rows_hbm, weight_hbm, source_hbm, inverse_hbm, coupling_hbm,
-    fwd_high_hbm, fwd_low_hbm, inv_high_hbm, inv_low_hbm,
-    values_out, spectrum_out,
+    fwd_high_hbm, fwd_low_hbm, inv_high_hbm, inv_low_hbm, step_hbm,
+    last_fwd_high_hbm, last_fwd_low_hbm, last_inv_high_hbm, last_inv_low_hbm,
+    sigma_out,
     less_ref, great_ref, partner_ref, rows_ref, weight_ref, source_ref, inverse_ref, coupling_ref,
-    fwd_high, fwd_low, inv_high, inv_low, load_sem,
-    swapped, first_send, first_recv, second_send, second_recv, third_send,
-    orbital_table, slab_high, slab_low, couple_high, couple_low,
+    fwd_high, fwd_low, inv_high, inv_low, half_step,
+    last_fwd_high, last_fwd_low, last_inv_high, last_inv_low, load_sem,
+    values, spectrum,
+    swapped, ordered, first_send, first_recv, second_send, second_recv, third_send,
+    orbital_table, slab_high, slab_low, couple_high, couple_low, lift_high, lift_low,
     steps, inbox, rest, rest_in, step_high, step_low, next_send, next_recv, twin_send, twin_recv,
     upward, offset, carried, arrived, across_send, across_recv,
     send_one, recv_one, send_two, recv_two, send_three, recv_three,
@@ -171,7 +237,31 @@
     orbitals = inverse_ref.shape[0]
     half, full = orbitals // 2, orbitals // 128 * 128
     core = lax.rem(me, 2)
+    in_upper = me >= peers // 2
+
+    def as_is(place):
+        return place
+
+    def mirrored(place):
+        return jnp.where(place < peers // 2, place, 3 * peers // 2 - 1 - place)
+
     twin = me + 1 - 2 * core
+
+    barrier = pltpu.get_barrier_semaphore()
+
+    def greet(n, _):
+        peer = lax.rem(me + far_first(peers, n), peers)
+        pl.semaphore_signal(barrier, inc=1, device_id={"energy": peer}, device_id_type=MESH)
+        return 0
+
+    lax.fori_loop(0, peers - 1, greet, 0)
+
+    for away in range(1, REACH + 1):
+        for there, other in ((section >= away, section - away), (section < sections - away, section + away)):
+
+            @pl.when(there)
+            def _(other=other):
+                pl.semaphore_signal(barrier, inc=1, device_id={"section": other}, device_id_type=MESH)
 
     loads = [
         pltpu.make_async_copy(source, target, load_sem.at[place])
@@ -180,44 +270,33 @@
             (weight_hbm, weight_ref), (source_hbm, source_ref), (inverse_hbm, inverse_ref),
             (coupling_hbm, coupling_ref), (fwd_high_hbm, fwd_high), (fwd_low_hbm, fwd_low),
             (inv_high_hbm, inv_high), (inv_low_hbm, inv_low),
+            (step_hbm, half_step),
+            (last_fwd_high_hbm, last_fwd_high), (last_fwd_low_hbm, last_fwd_low),
+            (last_inv_high_hbm, last_inv_high), (last_inv_low_hbm, last_inv_low),
         ))
     ]
     for load in loads:
         load.start()
 
-    barrier = pltpu.get_barrier_semaphore()
-
-    def greet(n, _):
-        peer = lax.rem(me + far_first(peers, n), peers)
-        pl.semaphore_signal(barrier, inc=1, device_id={"energy": peer}, device_id_type=MESH)
-        return 0
-
-    lax.fori_loop(0, peers - 1, greet, 0)
-
-    for away in range(1, REACH + 1):
-        for there, other in ((section >= away, section - away), (section < sections - away, section + away)):
-
-            @pl.when(there)
-            def _(other=other):
-                pl.semaphore_signal(barrier, inc=1, device_id={"section": other}, device_id_type=MESH)
-
-    loads[0].wait()
-    loads[1].wait()
-    loads[2].wait()
+    for load in loads[:3]:
+        load.wait()
 
     partner = partner_ref[...]
     partner_tile, partner_lane = partner // 128, partner % 128
-    for energy in range(16):
+    for place in range(16):
+        energy = pl.ds(pl.multiple_of(8 * jnp.where(in_upper, 15 - place, place), 8), 8)
+        lines = great_ref[energy, :]
         total = jnp.zeros((8, 128), F32)
         for tile in range(8):
-            line = jnp.broadcast_to(great_ref[8 * energy + tile : 8 * energy + tile + 1, :], (8, 128))
+            line = jnp.broadcast_to(lines[tile : tile + 1, :], (8, 128))
             total = jnp.where(partner_tile == tile, lane_take(line, partner_lane), total)
-        swapped[8 * energy : 8 * energy + 8, :] = total
+        swapped[8 * place : 8 * place + 8, :] = total
+        ordered[8 * place : 8 * place + 8, :] = less_ref[energy, :]
 
     for tile in range(8):
         parts = []
         for h in range(2):
-            for ref in (less_ref, swapped):
+            for ref in (ordered, swapped):
                 parts.append(ref[pl.ds(64 * h + tile, 8, stride=8), :])
         for b, part in enumerate(exchange_groups(parts)):
             first_send[4 * tile + b] = part
@@ -243,7 +322,7 @@
         rest[0, chunk] = fold_rest(own_half[chunk_rows(chunk)])
 
     pl.semaphore_wait(barrier, peers - 1 + jnp.minimum(section, REACH) + jnp.minimum(sections - 1 - section, REACH))
-    scatter_start(peers, me, first_send, first_recv, send_one, recv_one)
+    scatter_start(peers, me, first_send, first_recv, send_one, recv_one, as_is, mirrored)
 
     def rows_of(chunk):
         rows = chunk_rows(chunk)
@@ -322,40 +401,55 @@
         )
     source = source_ref[...]
     base = product(jnp.broadcast_to(source, (16, orbitals)), slab_high[...], slab_low[...], NT)
+    inverse_turned = dot(identity, slab_high[...], NT).astype(BF16), dot(identity, slab_low[...], NT).astype(BF16)
+    lift_high[...], lift_low[...] = split(
+        dot(inverse_turned[0], couple_high[...])
+        + dot(inverse_turned[0], couple_low[...])
+        + dot(inverse_turned[1], couple_high[...])
+    )
+    base_up = product(base, couple_high[...], couple_low[...], NN)
     grow(2, 0)
 
-    for load in loads[8:]:
+    for load in loads[8:13]:
         load.wait()
     wait_blocks(peers, first_recv, recv_one)
 
-    blocks = first_recv[...].reshape(peers * 8, 128)
-    low_lanes = lanes_of(blocks.shape) < 64
-    high = blocks.astype(BF16).astype(F32)
-    low = blocks - high
-    stacked = jnp.concatenate(
-        [
-            jnp.where(low_lanes, high, roll(low, 64)).astype(BF16),
-            jnp.where(low_lanes, roll(high, 64), low).astype(BF16),
-        ],
-        axis=0,
+    first = first_recv[: peers // 2].reshape(peers * 4, 128)
+    second = first_recv[peers // 2 :].reshape(peers * 4, 128)
+    low_lanes = lanes_of(first.shape) < 64
+
+    def parts_of(x):
+        high = x.astype(BF16).astype(F32)
+        low = x - high
+        left = jnp.where(low_lanes, high, roll(low, 64))
+        right = jnp.where(low_lanes, roll(high, 64), low)
+        return jnp.concatenate([left, right], axis=0).astype(BF16)
+
+    def forward(rows, x):
+        halves = dot(fwd_high[rows], x) + dot(fwd_low[rows], x)
+        return halves + roll(halves, 64)
+
+    cosines, sines = pl.ds(0, HALF), pl.ds(HALF, HALF)
+    cos_a, sin_a = forward(cosines, parts_of(first + second)), forward(sines, parts_of(first - second))
+    spectrum[cosines], spectrum[sines] = cos_a, sin_a
+    cos_b, sin_b = roll(cos_a, 96), roll(sin_a, 96)
+    real, turned = cos_a * cos_b + sin_a * sin_b, sin_a * cos_b - cos_a * sin_b
+    cos_half, sin_half = half_step[cosines], half_step[sines]
+    even, odd = backward(
+        inv_high, inv_low, real * cos_half - turned * sin_half, turned * cos_half + real * sin_half
     )
-    halves = dot(fwd_high[...], stacked) + dot(fwd_low[...], stacked)
-    spectrum = halves + roll(halves, 64)
-    spectrum_out[...] = spectrum
-    other = roll(spectrum, 96)
-    cos_a, sin_a, cos_b, sin_b = spectrum[:HALF], spectrum[HALF:], other[:HALF], other[HALF:]
-    crossed = jnp.concatenate([cos_a * cos_b + sin_a * sin_b, sin_a * cos_b - cos_a * sin_b], axis=0)
-    high = crossed.astype(BF16).astype(F32)
-    packed = jnp.where(lanes_of(crossed.shape) < 32, high, roll(crossed - high, 32)).astype(BF16)
-    halves = dot(inv_high[...], packed) + dot(inv_low[...], packed)
-    polar = halves + roll(halves, 96)
-    count = polar.shape[0] // 4
-    group = lanes_of((count, 128)) // 32
-    joined = polar[:count]
-    for q in range(1, 4):
-        joined = jnp.where(group == q, roll(polar[count * q : count * (q + 1)], 32 * q), joined)
-    second_send[...] = joined.reshape(peers, 4, 128)
-    scatter_start(peers, me, second_send, second_recv, send_two, recv_two)
+    group = lanes_of((peers * 2, 128)) // 32
+
+    def join(polar):
+        count = polar.shape[0] // 4
+        joined = polar[:count]
+        for q in range(1, 4):
+            joined = jnp.where(group == q, roll(polar[count * q : count * (q + 1)], 32 * q), joined)
+        return joined.reshape(peers // 2, 4, 128)
+
+    second_send[: peers // 2] = join(even + odd)
+    second_send[peers // 2 :] = join(even - odd)
+    scatter_start(peers, me, second_send, second_recv, send_two, recv_two, mirrored, as_is)
     grow(2, 1)
     grow(3, 0)
     gather(2)
@@ -370,8 +464,8 @@
         weighted.append(jnp.concatenate([one, two], axis=0) * weight_ref[tile : tile + 1, :])
     both = dot(jnp.concatenate(split(jnp.concatenate(weighted, axis=1)), axis=0), orbital_table[...], NT)
     local_pol = both[:16] + both[16:]
-    guess = base + product(local_pol * base, slab_high[...], slab_low[...], NT)
-    upward[...] = product(guess, couple_high[...], couple_low[...], NN)
+    spread = local_pol * base
+    upward[...] = base_up + product(spread, lift_high[...], lift_low[...], NN)
 
     def across(source, place, away):
         return pltpu.make_async_remote_copy(
@@ -391,8 +485,9 @@
     def _():
         shift.start()
 
+    guess = base + product(spread, slab_high[...], slab_low[...], NT)
+    partial = product(source + local_pol * guess, slab_high[...], slab_low[...], NT)
     grow(4, 0)
-    partial = source + local_pol * guess
 
     @pl.when(has_after)
     def _():
@@ -402,7 +497,7 @@
     def _():
         arrived[0] = jnp.zeros_like(upward)
 
-    offset[...] = product(partial + arrived[0], slab_high[...], slab_low[...], NT)
+    offset[...] = partial + product(arrived[0], slab_high[...], slab_low[...], NT)
     for away in range(1, REACH):
 
         @pl.when(section < sections - away)
@@ -441,7 +536,14 @@
         one, two = exchange_rows(piece[:8], piece[8:])
         for b, block in enumerate((one[:4], one[4:], two[:4], two[4:])):
             third_send[4 * tile + b] = block
-    scatter_start(peers, me, third_send, values_out, send_three, recv_three)
+    scatter_start(peers, me, third_send, values, send_three, recv_three, as_is, mirrored)
+
+    for load in loads[13:]:
+        load.wait()
+    wait_blocks(peers, values, recv_three)
+    convolve(
+        values, spectrum, last_fwd_high, last_fwd_low, last_inv_high, last_inv_low, half_step, sigma_out
+    )
 
     @pl.when(has_before)
     def _():
@@ -471,50 +573,21 @@
     wait_blocks(peers, first_send, send_one)
     wait_blocks(peers, second_send, send_two)
     wait_blocks(peers, third_send, send_three)
-    wait_blocks(peers, values_out, recv_three)
-
-
-def last_kernel(values_ref, spectrum_ref, fwd_high, fwd_low, inv_high, inv_low, sigma_ref):
-    values = values_ref[...].reshape(values_ref.shape[0] * 4, 128)
-    lane = lanes_of(values.shape)
-    high = values.astype(BF16).astype(F32)
-    low = values - high
-    stacked = []
-    for q in range(4):
-        left = high if q == 0 else roll(high, 128 - 32 * q)
-        right = roll(low, (160 - 32 * q) % 128) if q != 1 else low
-        stacked.append(jnp.where(lane < 32, left, right).astype(BF16))
-    stacked = jnp.concatenate(stacked, axis=0)
-    halves = dot(fwd_high[...], stacked) + dot(fwd_low[...], stacked)
-    wave = halves + roll(halves, 96)
-    spectrum = spectrum_ref[...]
-    cos_a, sin_a, cos_w, sin_w = spectrum[:HALF], spectrum[HALF:], wave[:HALF], wave[HALF:]
-    crossed = jnp.concatenate([cos_a * cos_w - sin_a * sin_w, cos_a * sin_w + sin_a * cos_w], axis=0)
-    high = crossed.astype(BF16).astype(F32)
-    packed = jnp.where(lanes_of(crossed.shape) < 32, high, roll(crossed - high, 32)).astype(BF16)
-    halves = dot(inv_high[...], packed) + dot(inv_low[...], packed)
-    full = halves + roll(halves, 96)
-    sigma_ref[...] = jnp.transpose(full)[:32]
 
 
 def on_device(peers, sections, g_less, g_greater, partner, pair_rows, pair_weight, source, slab_inverse, coupling):
     own, _, columns = g_less.shape
     energies = own * peers
     orbitals = slab_inverse.shape[-1]
-    polar_times = energy_order(peers, own, 4) - energies // 2
-    sigma_times = np.arange(energies) + energies // 2
     vmem = pl.BlockSpec(memory_space=pltpu.VMEM)
     hbm = pl.BlockSpec(memory_space=pltpu.HBM)
     square = (orbitals, orbitals)
     strip = (own, orbitals)
-    values, spectrum = pl.pallas_call(
+    sigma = pl.pallas_call(
         functools.partial(main_kernel, peers, sections),
-        out_shape=(
-            jax.ShapeDtypeStruct((peers, 4, 128), F32),
-            jax.ShapeDtypeStruct((LENGTH, 128), F32),
-        ),
-        in_specs=[hbm] * 12,
-        out_specs=(vmem, vmem),
+        out_shape=pltpu.VMEM((columns // peers, energies), F32),
+        in_specs=[hbm] * 17,
+        out_specs=vmem,
         scratch_shapes=[
             pltpu.VMEM((128, 128), F32),
             pltpu.VMEM((128, 128), F32),
@@ -524,11 +597,19 @@
             pltpu.VMEM((1, orbitals), F32),
             pltpu.VMEM(square, F32),
             pltpu.VMEM(square, F32),
-            pltpu.VMEM((LENGTH, energies), BF16),
-            pltpu.VMEM((LENGTH, energies), BF16),
-            pltpu.VMEM((energies, LENGTH), BF16),
-            pltpu.VMEM((energies, LENGTH), BF16),
-            pltpu.SemaphoreType.DMA((12,)),
+            pltpu.VMEM((LENGTH, energies // 2), BF16),
+            pltpu.VMEM((LENGTH, energies // 2), BF16),
+            pltpu.VMEM((energies, HALF), BF16),
+            pltpu.VMEM((energies, HALF), BF16),
+            pltpu.VMEM((LENGTH, 128), F32),
+            pltpu.VMEM((LENGTH, energies // 2), BF16),
+            pltpu.VMEM((LENGTH, energies // 2), BF16),
+            pltpu.VMEM((energies, HALF), BF16),
+            pltpu.VMEM((energies, HALF), BF16),
+            pltpu.SemaphoreType.DMA((17,)),
+            pltpu.VMEM((peers, 4, 128), F32),
+            pltpu.VMEM((LENGTH, 128), F32),
+            pltpu.VMEM((128, 128), F32),
             pltpu.VMEM((128, 128), F32),
             pltpu.VMEM((peers, 8, 128), F32),
             pltpu.VMEM((peers, 8, 128), F32),
@@ -536,6 +617,8 @@
             pltpu.VMEM((peers, 4, 128), F32),
             pltpu.VMEM((peers, 4, 128), F32),
             pltpu.VMEM((orbitals, columns), BF16),
+            pltpu.VMEM(square, BF16),
+            pltpu.VMEM(square, BF16),
             pltpu.VMEM(square, BF16),
             pltpu.VMEM(square, BF16),
             pltpu.VMEM(square, BF16),
@@ -571,21 +654,11 @@
         source,
         slab_inverse[0],
         coupling[0],
-        *forward_table(energy_order(peers, own, 2)),
-        *inverse_table(polar_times, energies),
-    )
-    sigma = pl.pallas_call(
-        last_kernel,
-        out_shape=jax.ShapeDtypeStruct((columns // peers, energies), F32),
-        in_specs=[vmem] * 6,
-        out_specs=vmem,
-        compiler_params=pltpu.CompilerParams(vmem_limit_bytes=32 * 1024 * 1024),
-        name="convolution",
-    )(
-        values,
-        spectrum,
-        *forward_table(energy_order(peers, own, 4)),
-        *inverse_table(sigma_times, energies),
+        *forward_table(energy_order(peers, own, 2), energies),
+        *inverse_table(energy_order(peers, own, 4), energies),
+        half_steps(),
+        *forward_table(energy_order(peers, own, 4), energies),
+        *inverse_table(np.arange(energies // 2), energies),
     )
     return jnp.transpose(sigma)[:, None, :]
 

time: 64.6 us -> 59.9 us (0.927)
  Pallas kernels: 62.6 us -> 59.1 us
  local copies, waits for them, and re-layouts: 1.85 us -> 0.63 us
    pallas_call x1 -> x0, Pallas kernels: 2.88 us -> none  [on_device(): pl.pallas_call(last_kernel, out_shape=jax.ShapeDtypeStruct((columns // pe...]
    unnamed x12 -> x1, local copies, waits for them, and re-layouts: 1.85 us -> 0.63 us
where the time goes in v3:
time: 59.9 us; the launch traced here: 59.8 us
  Pallas kernels  59.1 us (99%)
  local copies, waits for them, and re-layouts  0.63 us (1%)
    pallas_call x1, Pallas kernels, on_device(): pl.pallas_call(functools.partial(main_kernel, peers, sections), out_shape...  59.1 us

profile of v3, /device:TPU:25, one launch (start us, length us, event | category | flops | bytes accessed | tf_op | source)
XLA Modules:
  0.0 59.8 jit_solution(10168703672468906937)
XLA Ops:
  0.0 59.1 %update.1 = f32[32,512]{1,0:T(8,128)S(1)} custom-call(f32[128,128]{1,0:T(8,128)} %bitcast.13, f32[128,128]{1,0:T(8,128)} %bitcast.14, s32[8,128]{1,0:T(8,128)} %bitcast.15, s32[8,128]{1,0:T(8,128)} %bitcast.16, f32[8,128]{1,0:T(8,128)} %bitcast.17, f32[1,416]{1,0:T(1,128)} %source_hbm.1, f32[416,416]{1,0:T(8,128)} %bitcast.11, f32[416,416]{1,0:T(8,128)} %bitcast.12, ...), custom_call_target="tpu_custom_call" | custom-call | tf_op jit(solution)/shard_map/update/pallas_call | solution.py:586
  59.1 0.6 %copy.19 = f32[512,1,32]{0,2,1:T(8,128)} copy(f32[512,1,32]{0,2,1:T(8,128)S(1)} %bitcast.10) | data formatting | bytes 131072

commit v4 on v3

--- a/solution.py
+++ b/solution.py
@@ -321,6 +321,12 @@
     for chunk in range(2):
         rest[0, chunk] = fold_rest(own_half[chunk_rows(chunk)])
 
+    for away in range(1, REACH):
+
+        @pl.when(section < away)
+        def _(away=away):
+            arrived[away] = jnp.zeros_like(arrived[away])
+
     pl.semaphore_wait(barrier, peers - 1 + jnp.minimum(section, REACH) + jnp.minimum(sections - 1 - section, REACH))
     scatter_start(peers, me, first_send, first_recv, send_one, recv_one, as_is, mirrored)
 
@@ -453,8 +459,6 @@
     grow(2, 1)
     grow(3, 0)
     gather(2)
-    grow(3, 1)
-    gather(3)
     wait_blocks(peers, second_recv, recv_two)
 
     weighted = []
@@ -485,8 +489,10 @@
     def _():
         shift.start()
 
+    grow(3, 1)
     guess = base + product(spread, slab_high[...], slab_low[...], NT)
     partial = product(source + local_pol * guess, slab_high[...], slab_low[...], NT)
+    gather(3)
     grow(4, 0)
 
     @pl.when(has_after)
@@ -506,13 +512,17 @@
 
     grow(4, 1)
     gather(4)
-    carried[...] = offset[...]
+    so_far = offset[...]
     for away in range(1, REACH):
 
         @pl.when(section >= away)
         def _(away=away):
             window[away - 1].wait_recv()
-            carried[...] += product(arrived[away], step_high[away - 1], step_low[away - 1], NN)
+
+        if away != 2:
+            for near in (1,) if away == 1 else (2, 3):
+                so_far += product(arrived[near], step_high[near - 1], step_low[near - 1], NN)
+    carried[...] = so_far
 
     @pl.when(section < REACH)
     def _():

time: 59.9 us -> 59.1 us (0.987)
  Pallas kernels: 59.1 us -> 58.3 us
    pallas_call x1, Pallas kernels: 59.1 us -> 58.3 us  [on_device(): pl.pallas_call(functools.partial(main_kernel, peers, sections), out_shape...]
where the time goes in v4:
time: 59.1 us; the launch traced here: 59 us
  Pallas kernels  58.3 us (99%)
  local copies, waits for them, and re-layouts  0.63 us (1%)
    pallas_call x1, Pallas kernels, on_device(): pl.pallas_call(functools.partial(main_kernel, peers, sections), out_shape...  58.3 us

profile of v4, /device:TPU:25, one launch (start us, length us, event | category | flops | bytes accessed | tf_op | source)
XLA Modules:
  0.0 59.0 jit_solution(10988811622249587896)
XLA Ops:
  0.0 58.3 %update.1 = f32[32,512]{1,0:T(8,128)S(1)} custom-call(f32[128,128]{1,0:T(8,128)} %bitcast.13, f32[128,128]{1,0:T(8,128)} %bitcast.14, s32[8,128]{1,0:T(8,128)} %bitcast.15, s32[8,128]{1,0:T(8,128)} %bitcast.16, f32[8,128]{1,0:T(8,128)} %bitcast.17, f32[1,416]{1,0:T(1,128)} %source_hbm.1, f32[416,416]{1,0:T(8,128)} %bitcast.11, f32[416,416]{1,0:T(8,128)} %bitcast.12, ...), custom_call_target="tpu_custom_call" | custom-call | tf_op jit(solution)/shard_map/update/pallas_call | solution.py:596
  58.3 0.6 %copy.19 = f32[512,1,32]{0,2,1:T(8,128)} copy(f32[512,1,32]{0,2,1:T(8,128)S(1)} %bitcast.10) | data formatting | bytes 131072

commit v5 on v4

--- a/solution.py
+++ b/solution.py
@@ -17,6 +17,7 @@
 LENGTH = 768
 HALF = LENGTH // 2
 REACH = 4
+CHUNKS = 3
 
 
 def two_parts(table):
@@ -134,7 +135,8 @@
 
 
 def chunk_rows(chunk):
-    return slice(0, 128) if chunk == 0 else slice(128, 208)
+    edges = (0, 80, 144, 208)
+    return slice(edges[chunk], edges[chunk + 1])
 
 
 def fold_rest(rows):
@@ -318,7 +320,7 @@
     turned = turned_high + turned_low
     steps[0, 0], steps[0, 1] = turned[:half], turned[half:]
     own_half = steps[0, core]
-    for chunk in range(2):
+    for chunk in range(CHUNKS):
         rest[0, chunk] = fold_rest(own_half[chunk_rows(chunk)])
 
     for away in range(1, REACH):
@@ -385,7 +387,7 @@
         to_twin(k, chunk).start()
 
     def gather(k):
-        for chunk in range(2):
+        for chunk in range(CHUNKS):
             to_twin(k, chunk).wait_recv()
         for part in range(2):
             rows = pl.ds(half * part, half)
@@ -396,7 +398,7 @@
         inbox[...] = jnp.zeros_like(inbox)
         rest_in[...] = jnp.zeros_like(rest_in)
 
-    for chunk in range(2):
+    for chunk in range(CHUNKS):
         pass_on(1, chunk)
 
     pair_rows = rows_ref[...]
@@ -457,7 +459,9 @@
     second_send[peers // 2 :] = join(even - odd)
     scatter_start(peers, me, second_send, second_recv, send_two, recv_two, mirrored, as_is)
     grow(2, 1)
+    grow(2, 2)
     grow(3, 0)
+    grow(3, 1)
     gather(2)
     wait_blocks(peers, second_recv, recv_two)
 
@@ -489,7 +493,7 @@
     def _():
         shift.start()
 
-    grow(3, 1)
+    grow(3, 2)
     guess = base + product(spread, slab_high[...], slab_low[...], NT)
     partial = product(source + local_pol * guess, slab_high[...], slab_low[...], NT)
     gather(3)
@@ -511,6 +515,7 @@
             window[away - 1].start()
 
     grow(4, 1)
+    grow(4, 2)
     gather(4)
     so_far = offset[...]
     for away in range(1, REACH):
@@ -569,7 +574,7 @@
     def _():
         sweep.wait_send()
 
-    for chunk in range(2):
+    for chunk in range(CHUNKS):
 
         @pl.when(has_after)
         def _(chunk=chunk):
@@ -635,14 +640,14 @@
             pltpu.VMEM(square, BF16),
             pltpu.VMEM((REACH, 2, orbitals // 2, orbitals), F32),
             pltpu.VMEM((REACH - 1, orbitals // 2, orbitals // 128 * 128), F32),
-            pltpu.VMEM((REACH - 1, 2, 32, 128), F32),
-            pltpu.VMEM((REACH - 1, 2, 32, 128), F32),
+            pltpu.VMEM((REACH - 1, CHUNKS, 32, 128), F32),
+            pltpu.VMEM((REACH - 1, CHUNKS, 32, 128), F32),
             pltpu.VMEM((REACH,) + square, BF16),
             pltpu.VMEM((REACH,) + square, BF16),
-            pltpu.SemaphoreType.DMA((REACH, 2, 2)),
-            pltpu.SemaphoreType.DMA((REACH, 2, 2)),
-            pltpu.SemaphoreType.DMA((REACH, 2)),
-            pltpu.SemaphoreType.DMA((REACH, 2)),
+            pltpu.SemaphoreType.DMA((REACH, CHUNKS, 2)),
+            pltpu.SemaphoreType.DMA((REACH, CHUNKS, 2)),
+            pltpu.SemaphoreType.DMA((REACH, CHUNKS)),
+            pltpu.SemaphoreType.DMA((REACH, CHUNKS)),
             pltpu.VMEM(strip, F32),
             pltpu.VMEM(strip, F32),
             pltpu.VMEM(strip, F32),

time: 59.1 us -> 61.8 us (1.046)
  Pallas kernels: 58.3 us -> 61 us
    pallas_call x1, Pallas kernels: 58.3 us -> 61 us  [on_device(): pl.pallas_call(functools.partial(main_kernel, peers, sections), out_shape...]
where the time goes in v5:
time: 61.8 us; the launch traced here: 61.7 us
  Pallas kernels  61 us (99%)
  local copies, waits for them, and re-layouts  0.63 us (1%)
    pallas_call x1, Pallas kernels, on_device(): pl.pallas_call(functools.partial(main_kernel, peers, sections), out_shape...  61 us

profile of v5, /device:TPU:25, one launch (start us, length us, event | category | flops | bytes accessed | tf_op | source)
XLA Modules:
  0.0 61.7 jit_solution(13114071372156904402)
XLA Ops:
  0.0 61.0 %update.1 = f32[32,512]{1,0:T(8,128)S(1)} custom-call(f32[128,128]{1,0:T(8,128)} %bitcast.13, f32[128,128]{1,0:T(8,128)} %bitcast.14, s32[8,128]{1,0:T(8,128)} %bitcast.15, s32[8,128]{1,0:T(8,128)} %bitcast.16, f32[8,128]{1,0:T(8,128)} %bitcast.17, f32[1,416]{1,0:T(1,128)} %source_hbm.1, f32[416,416]{1,0:T(8,128)} %bitcast.11, f32[416,416]{1,0:T(8,128)} %bitcast.12, ...), custom_call_target="tpu_custom_call" | custom-call | tf_op jit(solution)/shard_map/update/pallas_call | solution.py:601
  61.0 0.6 %copy.19 = f32[512,1,32]{0,2,1:T(8,128)} copy(f32[512,1,32]{0,2,1:T(8,128)S(1)} %bitcast.10) | data formatting | bytes 131072

commit v6 on v4

--- a/solution.py
+++ b/solution.py
@@ -361,8 +361,13 @@
             device_id_type=MESH,
         )
 
+    far_enough = section >= REACH
+
+    def sends(k):
+        return jnp.logical_and(has_after, section >= k) if k == REACH - 1 else has_after
+
     def pass_on(k, chunk):
-        @pl.when(has_after)
+        @pl.when(sends(k))
         def _():
             for copy in to_next(k, chunk):
                 copy.start()
@@ -493,7 +498,11 @@
     guess = base + product(spread, slab_high[...], slab_low[...], NT)
     partial = product(source + local_pol * guess, slab_high[...], slab_low[...], NT)
     gather(3)
-    grow(4, 0)
+
+    @pl.when(far_enough)
+    def _():
+        grow(4, 0)
+
 
     @pl.when(has_after)
     def _():
@@ -510,8 +519,12 @@
         def _(away=away):
             window[away - 1].start()
 
-    grow(4, 1)
-    gather(4)
+
+    @pl.when(far_enough)
+    def _():
+        grow(4, 1)
+        gather(4)
+
     so_far = offset[...]
     for away in range(1, REACH):
 
@@ -571,14 +584,19 @@
 
     for chunk in range(2):
 
-        @pl.when(has_after)
-        def _(chunk=chunk):
-            for k in range(1, REACH):
+        for k in range(1, REACH):
+
+            @pl.when(sends(k))
+            def _(k=k, chunk=chunk):
                 for copy in to_next(k, chunk):
                     copy.wait_send()
 
-        for k in range(2, REACH + 1):
+        for k in range(2, REACH):
             to_twin(k, chunk).wait_send()
+
+        @pl.when(far_enough)
+        def _(chunk=chunk):
+            to_twin(REACH, chunk).wait_send()
 
     wait_blocks(peers, first_send, send_one)
     wait_blocks(peers, second_send, send_two)

time: 59.1 us -> 59.1 us (level)
  no operation moved by 1% of the time
where the time goes in v6:
time: 59.1 us; the launch traced here: 59 us
  Pallas kernels  58.4 us (99%)
  local copies, waits for them, and re-layouts  0.63 us (1%)
    pallas_call x1, Pallas kernels, on_device(): pl.pallas_call(functools.partial(main_kernel, peers, sections), out_shape...  58.4 us

profile of v6, /device:TPU:25, one launch (start us, length us, event | category | flops | bytes accessed | tf_op | source)
XLA Modules:
  0.0 59.0 jit_solution(5187845807642959905)
XLA Ops:
  0.0 58.4 %update.1 = f32[32,512]{1,0:T(8,128)S(1)} custom-call(f32[128,128]{1,0:T(8,128)} %bitcast.13, f32[128,128]{1,0:T(8,128)} %bitcast.14, s32[8,128]{1,0:T(8,128)} %bitcast.15, s32[8,128]{1,0:T(8,128)} %bitcast.16, f32[8,128]{1,0:T(8,128)} %bitcast.17, f32[1,416]{1,0:T(1,128)} %source_hbm.1, f32[416,416]{1,0:T(8,128)} %bitcast.11, f32[416,416]{1,0:T(8,128)} %bitcast.12, ...), custom_call_target="tpu_custom_call" | custom-call | tf_op jit(solution)/shard_map/update/pallas_call | solution.py:614
  58.4 0.6 %copy.19 = f32[512,1,32]{0,2,1:T(8,128)} copy(f32[512,1,32]{0,2,1:T(8,128)S(1)} %bitcast.10) | data formatting | bytes 131072
